TPU v7x, 32 devices: a whole 2x2x4 slice. The times are simulated.
32 devices in a mesh: node: 16 (over z, y, x), col: 2 (over core).
Axes of the slice: x: 2, y: 2, z: 4, core: 2. Of those that a mesh axis runs over, the one named last changes fastest.
Arguments:
- x_t: bfloat16 [512, 8192], P('col', 'node'), may hold values from -6 to 6
- adj_tiles: bfloat16 [1024, 128, 128], P('node'), may hold values from -0.1875 to 0.1875
- tile_rows: int32 [1024], P('node'), may hold values from 0 to 3
- tile_cols: int32 [1024], P('node'), may hold values from 0 to 63, as said below
- tile_counts: int32 [16], P('node'), may hold values from 8 to 64, as said below
- w_first: bfloat16 [512, 512], P('col'), may hold values from -0.25 to 0.25
- b_first: float32 [512], P('col'), may hold values from -3 to 3
- w_second: bfloat16 [512, 512], P('col'), may hold values from -0.25 to 0.25
- b_second: float32 [512], P('col'), may hold values from -3 to 3
Outputs:
- out_t: float32 [512, 8192], P('col', 'node')
Inputs may be any that keep to these rules, and one draw needn't show every extreme that they name: `tile_cols`: column blocks q * 4 to q * 4 + 3 belong to device q of node. Among the live tiles of one device, at most 2 distinct column blocks belong to any one device, and every device's first 2 tiles name 2 distinct blocks of one device. `tile_counts`: some device has all 64 slots live.
All inputs are finite; a program needn't handle non-finite values.
Results may differ from a plain program's by a relative error of at most 0.004.
Values may be sent and summed in bfloat16 or wider, within the bound.
No kernel may reach another device: no remote copies, remote signals or barrier semaphores. Data moves between devices by JAX's collectives and lax.ppermute only.
A program may use at most 64 MiB of HBM per device.

v0:
```python
import functools

import jax
import jax.numpy as jnp
from jax import lax
from jax.experimental import pallas as pl
from jax.experimental.pallas import tpu as pltpu
from jax.sharding import PartitionSpec as P

BLK = 128
CAP = 2
GROUP = 8
NEAR = (0, 1, 2, 4)
PASSED = {7: 0, 4: 1, 1: 2, 2: 4}
STEPS = (7, 6, 3, 4, 5, 1, 2)
DEPTH = 4
RELAY_WORK = 50_000_000_000
WIDTH = 4
SMEM = pl.BlockSpec(memory_space=pltpu.SMEM)
VMEM = pl.BlockSpec(memory_space=pltpu.VMEM)
HBM = pl.BlockSpec(memory_space=pltpu.HBM)
PARAMS = pltpu.CompilerParams(vmem_limit_bytes=24 * 1024 * 1024)


def split(value, size):
    shift = size.bit_length() - 1
    if size == 1 << shift:
        return value >> shift, value & (size - 1)
    return lax.div(value, size), lax.rem(value, size)


def lowest(mask):
    return jnp.where(mask & 1 != 0, 0, jnp.where(mask & 2 != 0, 1, jnp.where(mask & 4 != 0, 2, 3)))


def highest(mask):
    return jnp.where(mask & 8 != 0, 3, jnp.where(mask & 4 != 0, 2, jnp.where(mask & 2 != 0, 1, 0)))


def owner_mask(words, owner, row_blocks):
    first = owner * row_blocks
    word = words[0]
    for at in range(1, len(words)):
        word = jnp.where(first >> 5 == at, words[at], word)
    return (word >> (first & 31)) & ((1 << row_blocks) - 1)


def words_kernel(count_ref, cols_ref, words_ref):
    live = count_ref[0]
    word_total = words_ref.shape[1]

    def step(slot, found):
        column = cols_ref[slot]
        bit = jnp.where(slot < live, 1 << (column & 31), 0)
        word = column >> 5
        return tuple(one | jnp.where(word == at, bit, 0) for at, one in enumerate(found))

    start = tuple(jnp.int32(0) for _ in range(word_total))
    found = lax.fori_loop(0, cols_ref.shape[0], step, start, unroll=8)
    for member in range(GROUP):
        for at in range(word_total):
            words_ref[member, at] = found[at]


def group_limit(tile_total, row_blocks):
    return -(-(tile_total // DEPTH + row_blocks) // WIDTH) * WIDTH


def list_kernel(cubes, row_blocks, count_ref, rows_ref, cols_ref, words_ref, lists, filled):
    tile_total = cols_ref.shape[0]
    node = lax.axis_index("node")
    cube, member = split(node, GROUP)
    words = [words_ref[0, at] for at in range(words_ref.shape[1])]
    limit = group_limit(tile_total, row_blocks)

    @pl.loop(0, limit)
    def _(group):
        lists[1 + group] = row_blocks
        for at in range(DEPTH):
            entry = 1 + limit + 2 * (group * DEPTH + at)
            lists[entry] = 0
            lists[entry + 1] = cubes * GROUP * CAP

    for row in range(row_blocks):
        filled[row] = 0

    @pl.loop(0, count_ref[0])
    def _(slot):
        row = rows_ref[slot]
        filled[row] = filled[row] + 1

    start = 0
    for row in range(row_blocks):
        groups, _ = split(filled[row] + DEPTH - 1, DEPTH)
        filled[row] = start * DEPTH

        @pl.loop(start, start + groups)
        def _(group):
            lists[1 + group] = row

        start = start + groups
    lists[0] = start

    @pl.loop(0, count_ref[0])
    def _(slot):
        owner, block = split(cols_ref[slot], row_blocks)
        home, other = split(owner, GROUP)
        unit = jnp.where(home >= cube, home - cube, home - cube + cubes)
        second = block != lowest(owner_mask(words, owner, row_blocks))
        row = rows_ref[slot]
        entry = 1 + limit + 2 * filled[row]
        filled[row] = filled[row] + 1
        lists[entry] = slot
        lists[entry + 1] = (unit * GROUP + (other ^ member)) * CAP + jnp.where(second, 1, 0)


def make_plan(tile_rows, tile_cols, tile_counts, cubes, row_blocks):
    tile_total = tile_cols.shape[0]
    word_total = -(-cubes * GROUP * row_blocks // 32)
    list_length = 1 + group_limit(tile_total, row_blocks) * (1 + 2 * DEPTH)
    own = pl.pallas_call(
        words_kernel,
        out_shape=jax.ShapeDtypeStruct((GROUP, word_total), jnp.int32),
        in_specs=[SMEM] * 2,
        out_specs=SMEM,
    )(tile_counts, tile_cols)
    lists = pl.pallas_call(
        functools.partial(list_kernel, cubes, row_blocks),
        out_shape=jax.ShapeDtypeStruct((list_length,), jnp.int32),
        in_specs=[SMEM] * 4,
        out_specs=SMEM,
        scratch_shapes=[pltpu.SMEM((row_blocks,), jnp.int32)],
    )(tile_counts, tile_rows, tile_cols, own)
    groups = [[cube * GROUP + member for member in range(GROUP)] for cube in range(cubes)]
    words = exchange(own, groups)
    return words, lists


def exchange(array, groups):
    return lax.all_to_all(
        array, "node", split_axis=0, concat_axis=0, tiled=True, axis_index_groups=groups
    )


def named_blocks(words_ref, member, owner, row_blocks):
    words = [words_ref[member, at] for at in range(words_ref.shape[1])]
    mask = owner_mask(words, owner, row_blocks)
    return [pl.multiple_of(block * BLK, BLK) for block in (lowest(mask), highest(mask))]


def pack_kernel(cubes, whole, messages, fetched, words_ref, *refs):
    held, refs = dict(zip(whole, refs)), refs[len(whole) :]
    total = len(messages)
    sent, packed, done = refs[:total], refs[total : 2 * total], refs[2 * total]
    row_blocks = held[whole[0]].shape[1] // BLK
    node = lax.axis_index("node")
    cube, member = split(node, GROUP)

    def fill(target, other, unit, source):
        owner = split(cube + unit, cubes)[1] * GROUP + (member ^ source)
        for slot, lane in enumerate(named_blocks(words_ref, other, owner, row_blocks)):
            target[slot] = held[unit, source][:, pl.ds(lane, BLK)]

    if fetched:
        own, held[0, 0] = held[0, 0], refs[-1]
        fetch = pltpu.make_async_copy(own, held[0, 0], done.at[total])
        fetch.start()
    copies = []
    for at, (step, sources) in reversed(list(enumerate(messages))):
        for part, (unit, source) in reversed(list(enumerate(sources))):
            if fetched and (unit, source) == (0, 0):
                fetch.wait()
            fill(packed[at].at[part], member ^ step, unit, source)
        copies.append(pltpu.make_async_copy(packed[at], sent[at], done.at[at]))
        copies[-1].start()
    for copy in copies:
        copy.wait()


def pack(cubes, words, held, messages, fetched, work):
    feat_local, nodes_local = next(iter(held.values())).shape
    shapes = [(len(sources), CAP, feat_local, BLK) for _, sources in messages]
    scratch = [pltpu.VMEM(shape, jnp.bfloat16) for shape in shapes]
    scratch += [pltpu.SemaphoreType.DMA((len(shapes) + 1,))]
    if fetched:
        scratch += [pltpu.VMEM((feat_local, nodes_local), jnp.bfloat16)]
        held = {**held, (0, 0): in_hbm(held[0, 0])}
    return pl.pallas_call(
        functools.partial(pack_kernel, cubes, tuple(held), messages, fetched),
        out_shape=[pltpu.HBM(shape, jnp.bfloat16) for shape in shapes],
        in_specs=[SMEM] + [HBM if fetched and at == (0, 0) else VMEM for at in held],
        out_specs=[HBM] * len(shapes),
        scratch_shapes=scratch,
        compiler_params=PARAMS,
        cost_estimate=pl.CostEstimate(flops=work, bytes_accessed=0, transcendentals=0),
    )(words, *held.values())


def in_hbm(array):
    return pltpu.with_memory_space_constraint(array, pltpu.HBM)


def keep_kernel(cubes, whole, words_ref, *refs):
    held, kept = refs[:-1], refs[-1]
    row_blocks = held[0].shape[1] // BLK
    node = lax.axis_index("node")
    cube, member = split(node, GROUP)
    for at, (unit, source) in enumerate(whole):
        owner = split(cube + unit, cubes)[1] * GROUP + (member ^ source)
        for slot, lane in enumerate(named_blocks(words_ref, member, owner, row_blocks)):
            kept[at, slot] = held[at][:, pl.ds(lane, BLK)]


def keep(cubes, words, held):
    shape = (len(held), CAP, held[0, 0].shape[0], BLK)
    return pl.pallas_call(
        functools.partial(keep_kernel, cubes, tuple(held)),
        out_shape=jax.ShapeDtypeStruct(shape, jnp.bfloat16),
        in_specs=[SMEM] + [VMEM] * len(held),
        out_specs=VMEM,
        compiler_params=PARAMS,
    )(words, *held.values())


def aggregate_kernel(cubes, limit, messages, fetched, lists_hbm, tiles, *refs):
    received, refs = refs[: len(messages)], refs[len(messages) :]
    out_ref, lists, blocks, total, done = refs[:5]
    pairs = [(lists_hbm, lists)]
    if fetched:
        pairs.append((tiles, refs[5]))
        tiles = refs[5]
    for (step, sources, far), array in zip(messages, received):
        for part, (unit, source) in enumerate(sources if far else ()):
            place = (unit * GROUP + (step ^ source)) * CAP
            pairs.append((array.at[part], blocks.at[place : place + CAP]))
    copies = [pltpu.make_async_copy(*pair, done.at[at]) for at, pair in enumerate(pairs)]
    for copy in copies:
        copy.start()
    total[...] = jnp.zeros_like(total)
    blocks[cubes * GROUP * CAP] = jnp.zeros_like(blocks[cubes * GROUP * CAP])
    for (step, sources, far), array in zip(messages, received):
        for part, (unit, source) in enumerate(() if far else sources):
            place = (unit * GROUP + (step ^ source)) * CAP
            blocks[place : place + CAP] = array[part]
    for copy in copies:
        copy.wait()

    @pl.loop(0, split(lists[0] + WIDTH - 1, WIDTH)[0])
    def _(loop_step):
        sums = []
        for wide in range(WIDTH):
            group = loop_step * WIDTH + wide
            left, right = [], []
            for at in range(DEPTH):
                entry = 1 + limit + 2 * (group * DEPTH + at)
                left.append(blocks[lists[entry + 1]])
                right.append(tiles[lists[entry]])
            summed = lax.dot_general(
                jnp.concatenate(left, axis=1),
                jnp.concatenate(right, axis=1),
                (((1,), (1,)), ((), ())),
                preferred_element_type=jnp.float32,
            )
            sums.append((lists[1 + group], summed))
        for row, summed in sums:
            total[row] += summed

    for row in range(out_ref.shape[1] // BLK):
        out_ref[:, row * BLK : (row + 1) * BLK] = total[row].astype(out_ref.dtype)


def aggregate(cubes, messages, fetched, lists, adj_tiles, received, nodes_local):
    feat_local = received[0].shape[2]
    row_blocks = nodes_local // BLK
    limit = group_limit(adj_tiles.shape[0], row_blocks)
    operands = [in_hbm(adj_tiles) if fetched else adj_tiles]
    operands += [in_hbm(one) if far else one for one, (_, _, far) in zip(received, messages)]
    spaces = [HBM if fetched else VMEM] + [HBM if far else VMEM for _, _, far in messages]
    scratch = [
        pltpu.SMEM(lists.shape, jnp.int32),
        pltpu.VMEM((cubes * GROUP * CAP + 1, feat_local, BLK), jnp.bfloat16),
        pltpu.VMEM((row_blocks + 1, feat_local, BLK), jnp.float32),
        pltpu.SemaphoreType.DMA((2 + cubes * GROUP,)),
    ]
    if fetched:
        scratch.append(pltpu.VMEM(adj_tiles.shape, jnp.bfloat16))
    return pl.pallas_call(
        functools.partial(aggregate_kernel, cubes, limit, messages, fetched),
        out_shape=jax.ShapeDtypeStruct((feat_local, nodes_local), jnp.bfloat16),
        in_specs=[HBM] + spaces,
        out_specs=VMEM,
        scratch_shapes=scratch,
        compiler_params=PARAMS,
        cost_estimate=pl.CostEstimate(
            flops=2 * adj_tiles.shape[0] * feat_local * BLK * BLK,
            bytes_accessed=2 * sum(one.size for one in operands),
            transcendentals=0,
        ),
    )(in_hbm(lists), *operands)


def gather_sums(feat_t, adj_tiles, plan, cubes, by_planes):
    words, lists = plan
    nodes = cubes * GROUP

    def to_member(array, step):
        return lax.ppermute(array, "node", [(n, n ^ step) for n in range(nodes)])

    relayed = {
        (unit, 0): lax.ppermute(
            feat_t, "node", [(n, (n - unit * GROUP) % nodes) for n in range(nodes)]
        )
        for unit in range(1, cubes)
    }
    if by_planes:
        held = {(0, 0): feat_t, **relayed}
        held.update({(unit, 4): to_member(array, 4) for (unit, _), array in held.items()})
        batches = [
            ([(0, 0)], 0),
            ([(0, 4)] + list(relayed), RELAY_WORK),
            ([(unit, 4) for unit, _ in relayed], RELAY_WORK),
        ]
        messages, received = [], []
        for number, (sources, work) in enumerate(batches):
            batch = [(step, sources) for step in (3, 1, 2, 0)]
            array = {at: held[at] for at in sources}
            sent = pack(cubes, words, array, batch, False, work)
            for one, (step, _) in zip(sent, batch):
                messages.append((step, sources, number == 0 or step == 0))
                received.append(to_member(one, step) if step else one)
    else:
        near = {(0, step): to_member(feat_t, step) if step else feat_t for step in NEAR}
        held = {**relayed, **near}
        batch = [
            (step, ([(0, PASSED[step])] if step in PASSED else []) + list(relayed))
            for step in STEPS
        ]
        sent = pack(cubes, words, held, batch, True, 0)
        received = [to_member(one, step) for one, (step, _) in zip(sent, batch)]
        received.append(keep(cubes, words, held))
        messages = [(*one, False) for one in batch] + [(0, list(held), False)]
    local = aggregate(
        cubes, messages, not by_planes, lists, adj_tiles, received, feat_t.shape[1]
    )
    return lax.all_gather(local, "col", axis=0, tiled=True)


def dense_kernel(weight, aggregated, bias, out_ref):
    out_ref[...] = (
        jnp.dot(weight[...], aggregated[...], preferred_element_type=jnp.float32) + bias[...]
    )


def dense(weight, aggregated, bias):
    return pl.pallas_call(
        dense_kernel,
        out_shape=jax.ShapeDtypeStruct((weight.shape[0], aggregated.shape[1]), jnp.float32),
        in_specs=[VMEM] * 3,
        out_specs=VMEM,
        compiler_params=PARAMS,
        cost_estimate=pl.CostEstimate(
            flops=2 * weight.size * aggregated.shape[1],
            bytes_accessed=2 * (weight.size + 3 * aggregated.size),
            transcendentals=0,
        ),
    )(weight, aggregated, bias[:, None])


def body(x_t, adj_tiles, tile_rows, tile_cols, tile_counts, w_first, b_first, w_second, b_second):
    cubes = lax.axis_size("node") // GROUP
    plan = make_plan(tile_rows, tile_cols, tile_counts, cubes, x_t.shape[1] // BLK)
    y_first = gather_sums(x_t, adj_tiles, plan, cubes, False)
    z_first = jnp.dot(w_first, y_first, preferred_element_type=jnp.float32) + b_first[:, None]
    h_first = jnp.maximum(z_first, 0.0).astype(jnp.bfloat16)
    y_second = gather_sums(h_first, adj_tiles, plan, cubes, True)
    return dense(w_second, y_second, b_second)


def solution(mesh):
    return jax.shard_map(
        body,
        mesh=mesh,
        in_specs=(
            P("col", "node"),
            P("node", None, None),
            P("node"),
            P("node"),
            P("node"),
            P("col", None),
            P("col"),
            P("col", None),
            P("col"),
        ),
        out_specs=P("col", "node"),
        check_vma=False,
    )
```

profile of v0, /device:TPU:0, one launch (start us, length us, event | category | flops | bytes accessed | tf_op | source)
XLA Modules:
  0.0 93.7 jit_solution(11201762464064727620)
XLA Ops:
  0.0 4.0 %collective-permute-start = (bf16[256,512]{1,0:T(8,128)(2,1)}, bf16[256,512]{1,0:T(8,128)(2,1)S(1)}, u32[]{:S(2)}, u32[]{:S(2)}) collective-permute-start(bf16[256,512]{1,0:T(8,128)(2,1)} %refs_1_.3), channel_id=1, source_target_pairs={{0,16},{2,18},{4,20},{6,22},{8,24},{10,26},{12,28},{14,30},{16,0},... | collective-permute-start | bytes 786440 | tf_op jit(solution)/shard_map/ppermute | solution.py:310
  4.0 1.5 %collective-permute-start.1 = (bf16[256,512]{1,0:T(8,128)(2,1)}, bf16[256,512]{1,0:T(8,128)(2,1)S(1)}, u32[]{:S(2)}, u32[]{:S(2)}) collective-permute-start(bf16[256,512]{1,0:T(8,128)(2,1)} %refs_1_.3), channel_id=1, source_target_pairs={{0,2},{2,0},{4,6},{6,4},{8,10},{10,8},{12,14},{14,12},{16,18},{18,... | collective-permute-start | bytes 786440 | tf_op jit(solution)/shard_map/ppermute | solution.py:307
  5.5 1.5 %collective-permute-start.2 = (bf16[256,512]{1,0:T(8,128)(2,1)}, bf16[256,512]{1,0:T(8,128)(2,1)S(1)}, u32[]{:S(2)}, u32[]{:S(2)}) collective-permute-start(bf16[256,512]{1,0:T(8,128)(2,1)} %refs_1_.3), channel_id=1, source_target_pairs={{0,4},{2,6},{4,0},{6,2},{8,12},{10,14},{12,8},{14,10},{16,20},{18,... | collective-permute-start | bytes 786440 | tf_op jit(solution)/shard_map/ppermute | solution.py:307
  7.1 1.6 %collective-permute-start.3 = (bf16[256,512]{1,0:T(8,128)(2,1)}, bf16[256,512]{1,0:T(8,128)(2,1)S(1)}, u32[]{:S(2)}, u32[]{:S(2)}) collective-permute-start(bf16[256,512]{1,0:T(8,128)(2,1)} %refs_1_.3), channel_id=1, source_target_pairs={{0,8},{2,10},{4,12},{6,14},{8,0},{10,2},{12,4},{14,6},{16,24},{18,... | collective-permute-start | bytes 786440 | tf_op jit(solution)/shard_map/ppermute | solution.py:307
  9.3 1.5 %shard_map.91.words_ref = s32[8,2]{1,0:T(8,128)} custom-call(s32[1]{0:T(128)S(6)} %copy.38.count_ref, s32[64]{0:T(128)} %cols_ref.3), custom_call_target="tpu_custom_call" | custom-call | tf_op jit(solution)/shard_map/pallas_call | solution.py:121
  10.8 8.7 %all_to_all.11 = s32[8,1,2]{2,1,0:T(1,128)S(1)} all-to-all(s32[8,1,2]{2,1,0:T(1,128)} %bitcast.9), channel_id=1, replica_groups={{0,2,4,6,8,10,12,14},{16,18,20,22,24,26,28,30},{1,3,5,7,9,11,13,15},{17..., dimensions={0} | all-to-all | bytes 128 | tf_op jit(solution)/shard_map/all_to_all | solution.py:140
  19.8 2.4 %shard_map.93 = (bf16[2,2,256,128]{3,2,1,0:T(8,128)(2,1)}, bf16[1,2,256,128]{3,2,1,0:T(8,128)(2,1)}, bf16[1,2,256,128]{3,2,1,0:T(8,128)(2,1)}, bf16[2,2,256,128]...) custom-call(s32[8,2]{1,0:T(8,128)S(1)} %copy.31.words_ref, ...), custom_call_target="tpu_custom_call" | custom-call | tf_op jit(solution)/shard_map/pallas_call | solution.py:188
  22.8 2.6 %collective-permute-start.4 = (bf16[2,2,256,128]{3,2,1,0:T(8,128)(2,1)}, bf16[2,2,256,128]{3,2,1,0:T(8,128)(2,1)S(1)}, u32[]{:S(2)}, u32[]{:S(2)}) collective-permute-start(bf16[2,2,256,128]{3,2,1,0:T(8,128)(2,1)} %get-tuple-element.24), channel_id=1, source_target_pairs={{0,14},{2,12},{4,10},{6,8},{8,6},{10,4},{12,2},{14,0},{16,30},{18,... | collective-permute-start | bytes 786440 | tf_op jit(solution)/shard_map/ppermute | solution.py:307
  28.3 2.3 %collective-permute-done.5.refs_1_ = bf16[1,2,256,128]{3,2,1,0:T(8,128)(2,1)S(1)} collective-permute-done((bf16[1,2,256,128]{3,2,1,0:T(8,128)(2,1)}, bf16[1,2,256,128]{3,2,1,0:T(8,128)(2,1)S(1)}, u32[]{:S(2)}, u32[]{:S(2)}) %collective-permute-start.5) | collective-permute-done | bytes 131104 | tf_op jit(solution)/shard_map/ppermute | solution.py:307
  31.4 5.0 %collective-permute-done.6.refs_2_ = bf16[1,2,256,128]{3,2,1,0:T(8,128)(2,1)S(1)} collective-permute-done((bf16[1,2,256,128]{3,2,1,0:T(8,128)(2,1)}, bf16[1,2,256,128]{3,2,1,0:T(8,128)(2,1)S(1)}, u32[]{:S(2)}, u32[]{:S(2)}) %collective-permute-start.6) | collective-permute-done | bytes 131104 | tf_op jit(solution)/shard_map/ppermute | solution.py:307
  37.8 2.5 %shard_map.92.lists_hbm = s32[181]{0:T(256)} custom-call(s32[1]{0:T(128)S(6)} %copy.38.count_ref, s32[64]{0:T(128)} %rows_ref.1, s32[64]{0:T(128)} %cols_ref.3, s32[8,2]{1,0:T(8,128)} %shard_map.91.words_ref), custom_call_target="tpu_custom_call" | custom-call | tf_op jit(solution)/shard_map/pallas_call | solution.py:127
  43.8 3.1 %shard_map.95 = bf16[256,512]{1,0:T(8,128)(2,1)S(1)} custom-call(s32[181]{0:T(256)} %shard_map.92.lists_hbm, bf16[64,128,128]{2,1,0:T(8,128)(2,1)} %tiles.3, bf16[2,2,256,128]{3,2,1,0:T(8,128)(2,1)S(1)} %collective-permute-done.4.refs_0_, bf16[1,2,256,128]{3,2,1,0:T(8,128)(2,1)S(1)} %collective-permute-done.5.refs_1_, ...), custom_call_target="tpu_custom_call" | custom-call | flops 536870912 | bytes 4194304 | tf_op jit(solution)/shard_map/pallas_call | solution.py:287
  46.9 2.2 %all_gather.6 = bf16[512,512]{1,0:T(8,128)(2,1)S(1)} all-gather(bf16[256,512]{1,0:T(8,128)(2,1)S(1)} %shard_map.95), channel_id=1, replica_groups=mesh['node'=16,'col'=2] {'col'}, dimensions={0}, use_global_device_ids=true | all-gather | bytes 786432 | tf_op jit(solution)/shard_map/all_gather | solution.py:345
  50.8 1.9 %collective-permute-start.14 = (bf16[256,512]{1,0:T(8,128)(2,1)S(1)}, bf16[256,512]{1,0:T(8,128)(2,1)S(1)}, u32[]{:S(2)}, u32[]{:S(2)}) collective-permute-start(bf16[256,512]{1,0:T(8,128)(2,1)S(1)} %fusion.2.refs_0_), channel_id=1, source_target_pairs={{0,8},{2,10},{4,12},{6,14},{8,0},{10,2},{12,4},{14,6},{16,24},{18,... | collective-permute-start | bytes 786440 | tf_op jit(solution)/shard_map/ppermute | solution.py:307
  55.1 1.8 %collective-permute-start.12 = (bf16[1,2,256,128]{3,2,1,0:T(8,128)(2,1)}, bf16[1,2,256,128]{3,2,1,0:T(8,128)(2,1)S(1)}, u32[]{:S(2)}, u32[]{:S(2)}) collective-permute-start(bf16[1,2,256,128]{3,2,1,0:T(8,128)(2,1)} %get-tuple-element.32), channel_id=1, source_target_pairs={{0,2},{2,0},{4,6},{6,4},{8,10},{10,8},{12,14},{14,12},{16,18},{18,... | collective-permute-start | bytes 393224 | tf_op jit(solution)/shard_map/ppermute | solution.py:307
  58.3 6.1 %collective-permute-done.15.refs_1_ = bf16[256,512]{1,0:T(8,128)(2,1)S(1)} collective-permute-done((bf16[256,512]{1,0:T(8,128)(2,1)S(1)}, bf16[256,512]{1,0:T(8,128)(2,1)S(1)}, u32[]{:S(2)}, u32[]{:S(2)}) %collective-permute-start.15) | collective-permute-done | bytes 262176 | tf_op jit(solution)/shard_map/ppermute | solution.py:310
  64.4 1.7 %shard_map.97 = (bf16[2,2,256,128]{3,2,1,0:T(8,128)(2,1)}, bf16[2,2,256,128]{3,2,1,0:T(8,128)(2,1)}, bf16[2,2,256,128]{3,2,1,0:T(8,128)(2,1)}, bf16[2,2,256,128]{3,2,1,0:T(8,128)(2,1)}) custom-call(s32[8,2]{1,0:T(8,128)S(1)} %copy.31.words_ref, bf16[256,512]{1,0:T(8,128)(2,1)S(1)} %collective-permute-done.14.refs_0_, ...), custom_call_target="tpu_custom_call" | custom-call | flops 49999998976 | tf_op jit(solution)/shard_map/pallas_call | solution.py:188
  66.1 2.7 %collective-permute-start.16 = (bf16[2,2,256,128]{3,2,1,0:T(8,128)(2,1)}, bf16[2,2,256,128]{3,2,1,0:T(8,128)(2,1)S(1)}, u32[]{:S(2)}, u32[]{:S(2)}) collective-permute-start(bf16[2,2,256,128]{3,2,1,0:T(8,128)(2,1)} %get-tuple-element.35), channel_id=1, source_target_pairs={{0,6},{2,4},{4,2},{6,0},{8,14},{10,12},{12,10},{14,8},{16,22},{18,... | collective-permute-start | bytes 786440 | tf_op jit(solution)/shard_map/ppermute | solution.py:307
  69.4 3.1 %collective-permute-done.19.refs_0_ = bf16[256,512]{1,0:T(8,128)(2,1)S(1)} collective-permute-done((bf16[256,512]{1,0:T(8,128)(2,1)S(1)}, bf16[256,512]{1,0:T(8,128)(2,1)S(1)}, u32[]{:S(2)}, u32[]{:S(2)}) %collective-permute-start.19) | collective-permute-done | bytes 262176 | tf_op jit(solution)/shard_map/ppermute | solution.py:307
  79.0 2.8 %collective-permute-done.17.refs_5_ = bf16[2,2,256,128]{3,2,1,0:T(8,128)(2,1)S(1)} collective-permute-done((bf16[2,2,256,128]{3,2,1,0:T(8,128)(2,1)}, bf16[2,2,256,128]{3,2,1,0:T(8,128)(2,1)S(1)}, u32[]{:S(2)}, u32[]{:S(2)}) %collective-permute-start.17) | collective-permute-done | bytes 262176 | tf_op jit(solution)/shard_map/ppermute | solution.py:307
  81.8 3.1 %collective-permute-done.18.refs_6_ = bf16[2,2,256,128]{3,2,1,0:T(8,128)(2,1)S(1)} collective-permute-done((bf16[2,2,256,128]{3,2,1,0:T(8,128)(2,1)}, bf16[2,2,256,128]{3,2,1,0:T(8,128)(2,1)S(1)}, u32[]{:S(2)}, u32[]{:S(2)}) %collective-permute-start.18) | collective-permute-done | bytes 262176 | tf_op jit(solution)/shard_map/ppermute | solution.py:307
  84.9 1.5 %collective-permute-done.21.refs_9_ = bf16[1,2,256,128]{3,2,1,0:T(8,128)(2,1)S(1)} collective-permute-done((bf16[1,2,256,128]{3,2,1,0:T(8,128)(2,1)}, bf16[1,2,256,128]{3,2,1,0:T(8,128)(2,1)S(1)}, u32[]{:S(2)}, u32[]{:S(2)}) %collective-permute-start.21) | collective-permute-done | bytes 131104 | tf_op jit(solution)/shard_map/ppermute | solution.py:307
  86.7 3.7 %shard_map.99 = bf16[256,512]{1,0:T(8,128)(2,1)S(1)} custom-call(s32[181]{0:T(256)} %shard_map.92.lists_hbm, bf16[64,128,128]{2,1,0:T(8,128)(2,1)S(1)} %copy-done.1, bf16[1,2,256,128]{3,2,1,0:T(8,128)(2,1)} %copy-done.4, bf16[1,2,256,128]{3,2,1,0:T(8,128)(2,1)} %copy-done.5, bf16[1,2,256,128]{3,2,1,0:T(8,128)(2,1)} %copy-done.6, ...), custom_call_target="tpu_custom_call" | custom-call | flops 536870912 | bytes 4194304 | tf_op jit(solution)/shard_map/pallas_call | solution.py:287
  90.5 2.2 %all_gather.7.aggregated = bf16[512,512]{1,0:T(8,128)(2,1)S(1)} all-gather(bf16[256,512]{1,0:T(8,128)(2,1)S(1)} %shard_map.99), channel_id=1, replica_groups=mesh['node'=16,'col'=2] {'col'}, dimensions={0}, use_global_device_ids=true | all-gather | bytes 786432 | tf_op jit(solution)/shard_map/all_gather | solution.py:345
  (57 shorter events, 23.5 us)
Async XLA Ops:
  0.0 49.1 %copy-start = (bf16[256,512]{1,0:T(8,128)(2,1)S(1)}, bf16[256,512]{1,0:T(8,128)(2,1)}, u32[]{:S(2)}) copy-start(bf16[256,512]{1,0:T(8,128)(2,1)} %param.14) | copy-start | bytes 786436
  0.0 19.7 %collective-permute-start = (bf16[256,512]{1,0:T(8,128)(2,1)}, bf16[256,512]{1,0:T(8,128)(2,1)S(1)}, u32[]{:S(2)}, u32[]{:S(2)}) collective-permute-start(bf16[256,512]{1,0:T(8,128)(2,1)} %refs_1_.3), channel_id=1, source_target_pairs={{0,16},{2,18},{4,20},{6,22},{8,24},{10,26},{12,28},{14,30},{16,0},... | collective-permute-start | bytes 786440 | tf_op jit(solution)/shard_map/ppermute | solution.py:310
  4.0 15.7 %collective-permute-start.1 = (bf16[256,512]{1,0:T(8,128)(2,1)}, bf16[256,512]{1,0:T(8,128)(2,1)S(1)}, u32[]{:S(2)}, u32[]{:S(2)}) collective-permute-start(bf16[256,512]{1,0:T(8,128)(2,1)} %refs_1_.3), channel_id=1, source_target_pairs={{0,2},{2,0},{4,6},{6,4},{8,10},{10,8},{12,14},{14,12},{16,18},{18,... | collective-permute-start | bytes 786440 | tf_op jit(solution)/shard_map/ppermute | solution.py:307
  5.5 14.2 %collective-permute-start.2 = (bf16[256,512]{1,0:T(8,128)(2,1)}, bf16[256,512]{1,0:T(8,128)(2,1)S(1)}, u32[]{:S(2)}, u32[]{:S(2)}) collective-permute-start(bf16[256,512]{1,0:T(8,128)(2,1)} %refs_1_.3), channel_id=1, source_target_pairs={{0,4},{2,6},{4,0},{6,2},{8,12},{10,14},{12,8},{14,10},{16,20},{18,... | collective-permute-start | bytes 786440 | tf_op jit(solution)/shard_map/ppermute | solution.py:307
  7.1 12.7 %collective-permute-start.3 = (bf16[256,512]{1,0:T(8,128)(2,1)}, bf16[256,512]{1,0:T(8,128)(2,1)S(1)}, u32[]{:S(2)}, u32[]{:S(2)}) collective-permute-start(bf16[256,512]{1,0:T(8,128)(2,1)} %refs_1_.3), channel_id=1, source_target_pairs={{0,8},{2,10},{4,12},{6,14},{8,0},{10,2},{12,4},{14,6},{16,24},{18,... | collective-permute-start | bytes 786440 | tf_op jit(solution)/shard_map/ppermute | solution.py:307
  22.1 8.5 %collective-permute-start.5 = (bf16[1,2,256,128]{3,2,1,0:T(8,128)(2,1)}, bf16[1,2,256,128]{3,2,1,0:T(8,128)(2,1)S(1)}, u32[]{:S(2)}, u32[]{:S(2)}) collective-permute-start(bf16[1,2,256,128]{3,2,1,0:T(8,128)(2,1)} %get-tuple-element.25), channel_id=1, source_target_pairs={{0,12},{2,14},{4,8},{6,10},{8,4},{10,6},{12,0},{14,2},{16,28},{18,... | collective-permute-start | bytes 393224 | tf_op jit(solution)/shard_map/ppermute | solution.py:307
  22.8 19.8 %collective-permute-start.4 = (bf16[2,2,256,128]{3,2,1,0:T(8,128)(2,1)}, bf16[2,2,256,128]{3,2,1,0:T(8,128)(2,1)S(1)}, u32[]{:S(2)}, u32[]{:S(2)}) collective-permute-start(bf16[2,2,256,128]{3,2,1,0:T(8,128)(2,1)} %get-tuple-element.24), channel_id=1, source_target_pairs={{0,14},{2,12},{4,10},{6,8},{8,6},{10,4},{12,2},{14,0},{16,30},{18,... | collective-permute-start | bytes 786440 | tf_op jit(solution)/shard_map/ppermute | solution.py:307
  25.4 11.0 %collective-permute-start.6 = (bf16[1,2,256,128]{3,2,1,0:T(8,128)(2,1)}, bf16[1,2,256,128]{3,2,1,0:T(8,128)(2,1)S(1)}, u32[]{:S(2)}, u32[]{:S(2)}) collective-permute-start(bf16[1,2,256,128]{3,2,1,0:T(8,128)(2,1)} %get-tuple-element.26), channel_id=1, source_target_pairs={{0,6},{2,4},{4,2},{6,0},{8,14},{10,12},{12,10},{14,8},{16,22},{18,... | collective-permute-start | bytes 393224 | tf_op jit(solution)/shard_map/ppermute | solution.py:307
  26.9 15.7 %collective-permute-start.7 = (bf16[2,2,256,128]{3,2,1,0:T(8,128)(2,1)}, bf16[2,2,256,128]{3,2,1,0:T(8,128)(2,1)S(1)}, u32[]{:S(2)}, u32[]{:S(2)}) collective-permute-start(bf16[2,2,256,128]{3,2,1,0:T(8,128)(2,1)} %get-tuple-element.27), channel_id=1, source_target_pairs={{0,8},{2,10},{4,12},{6,14},{8,0},{10,2},{12,4},{14,6},{16,24},{18,... | collective-permute-start | bytes 786440 | tf_op jit(solution)/shard_map/ppermute | solution.py:307
  27.1 16.6 %collective-permute-start.9 = (bf16[2,2,256,128]{3,2,1,0:T(8,128)(2,1)}, bf16[2,2,256,128]{3,2,1,0:T(8,128)(2,1)S(1)}, u32[]{:S(2)}, u32[]{:S(2)}) collective-permute-start(bf16[2,2,256,128]{3,2,1,0:T(8,128)(2,1)} %get-tuple-element.29), channel_id=1, source_target_pairs={{0,2},{2,0},{4,6},{6,4},{8,10},{10,8},{12,14},{14,12},{16,18},{18,... | collective-permute-start | bytes 786440 | tf_op jit(solution)/shard_map/ppermute | solution.py:307
  30.6 13.1 %collective-permute-start.10 = (bf16[2,2,256,128]{3,2,1,0:T(8,128)(2,1)}, bf16[2,2,256,128]{3,2,1,0:T(8,128)(2,1)S(1)}, u32[]{:S(2)}, u32[]{:S(2)}) collective-permute-start(bf16[2,2,256,128]{3,2,1,0:T(8,128)(2,1)} %get-tuple-element.30), channel_id=1, source_target_pairs={{0,4},{2,6},{4,0},{6,2},{8,12},{10,14},{12,8},{14,10},{16,20},{18,... | collective-permute-start | bytes 786440 | tf_op jit(solution)/shard_map/ppermute | solution.py:307
  36.4 6.2 %collective-permute-start.8 = (bf16[1,2,256,128]{3,2,1,0:T(8,128)(2,1)}, bf16[1,2,256,128]{3,2,1,0:T(8,128)(2,1)S(1)}, u32[]{:S(2)}, u32[]{:S(2)}) collective-permute-start(bf16[1,2,256,128]{3,2,1,0:T(8,128)(2,1)} %get-tuple-element.28), channel_id=1, source_target_pairs={{0,10},{2,8},{4,14},{6,12},{8,2},{10,0},{12,6},{14,4},{16,26},{18,... | collective-permute-start | bytes 393224 | tf_op jit(solution)/shard_map/ppermute | solution.py:307
  49.4 15.0 %collective-permute-start.15 = (bf16[256,512]{1,0:T(8,128)(2,1)S(1)}, bf16[256,512]{1,0:T(8,128)(2,1)S(1)}, u32[]{:S(2)}, u32[]{:S(2)}) collective-permute-start(bf16[256,512]{1,0:T(8,128)(2,1)S(1)} %fusion.2.refs_0_), channel_id=1, source_target_pairs={{0,16},{2,18},{4,20},{6,22},{8,24},{10,26},{12,28},{14,30},{16,0},... | collective-permute-start | bytes 786440 | tf_op jit(solution)/shard_map/ppermute | solution.py:310
  50.8 13.7 %collective-permute-start.14 = (bf16[256,512]{1,0:T(8,128)(2,1)S(1)}, bf16[256,512]{1,0:T(8,128)(2,1)S(1)}, u32[]{:S(2)}, u32[]{:S(2)}) collective-permute-start(bf16[256,512]{1,0:T(8,128)(2,1)S(1)} %fusion.2.refs_0_), channel_id=1, source_target_pairs={{0,8},{2,10},{4,12},{6,14},{8,0},{10,2},{12,4},{14,6},{16,24},{18,... | collective-permute-start | bytes 786440 | tf_op jit(solution)/shard_map/ppermute | solution.py:307
  54.1 14.6 %collective-permute-start.11 = (bf16[1,2,256,128]{3,2,1,0:T(8,128)(2,1)}, bf16[1,2,256,128]{3,2,1,0:T(8,128)(2,1)S(1)}, u32[]{:S(2)}, u32[]{:S(2)}) collective-permute-start(bf16[1,2,256,128]{3,2,1,0:T(8,128)(2,1)} %get-tuple-element.31), channel_id=1, source_target_pairs={{0,6},{2,4},{4,2},{6,0},{8,14},{10,12},{12,10},{14,8},{16,22},{18,... | collective-permute-start | bytes 393224 | tf_op jit(solution)/shard_map/ppermute | solution.py:307
  55.1 20.2 %collective-permute-start.12 = (bf16[1,2,256,128]{3,2,1,0:T(8,128)(2,1)}, bf16[1,2,256,128]{3,2,1,0:T(8,128)(2,1)S(1)}, u32[]{:S(2)}, u32[]{:S(2)}) collective-permute-start(bf16[1,2,256,128]{3,2,1,0:T(8,128)(2,1)} %get-tuple-element.32), channel_id=1, source_target_pairs={{0,2},{2,0},{4,6},{6,4},{8,10},{10,8},{12,14},{14,12},{16,18},{18,... | collective-permute-start | bytes 393224 | tf_op jit(solution)/shard_map/ppermute | solution.py:307
  56.9 19.8 %collective-permute-start.13 = (bf16[1,2,256,128]{3,2,1,0:T(8,128)(2,1)}, bf16[1,2,256,128]{3,2,1,0:T(8,128)(2,1)S(1)}, u32[]{:S(2)}, u32[]{:S(2)}) collective-permute-start(bf16[1,2,256,128]{3,2,1,0:T(8,128)(2,1)} %get-tuple-element.33), channel_id=1, source_target_pairs={{0,4},{2,6},{4,0},{6,2},{8,12},{10,14},{12,8},{14,10},{16,20},{18,... | collective-permute-start | bytes 393224 | tf_op jit(solution)/shard_map/ppermute | solution.py:307
  64.4 8.1 %collective-permute-start.19 = (bf16[256,512]{1,0:T(8,128)(2,1)S(1)}, bf16[256,512]{1,0:T(8,128)(2,1)S(1)}, u32[]{:S(2)}, u32[]{:S(2)}) collective-permute-start(bf16[256,512]{1,0:T(8,128)(2,1)S(1)} %collective-permute-done.15.refs_1_), channel_id=1, source_target_pairs={{0,8},{2,10},{4,12},{6,14},{8,0},{10,2},{12,4},{14,6},{16,24},{18,... | collective-permute-start | bytes 786440 | tf_op jit(solution)/shard_map/ppermute | solution.py:307
  66.1 11.5 %collective-permute-start.16 = (bf16[2,2,256,128]{3,2,1,0:T(8,128)(2,1)}, bf16[2,2,256,128]{3,2,1,0:T(8,128)(2,1)S(1)}, u32[]{:S(2)}, u32[]{:S(2)}) collective-permute-start(bf16[2,2,256,128]{3,2,1,0:T(8,128)(2,1)} %get-tuple-element.35), channel_id=1, source_target_pairs={{0,6},{2,4},{4,2},{6,0},{8,14},{10,12},{12,10},{14,8},{16,22},{18,... | collective-permute-start | bytes 786440 | tf_op jit(solution)/shard_map/ppermute | solution.py:307
  69.4 12.3 %collective-permute-start.17 = (bf16[2,2,256,128]{3,2,1,0:T(8,128)(2,1)}, bf16[2,2,256,128]{3,2,1,0:T(8,128)(2,1)S(1)}, u32[]{:S(2)}, u32[]{:S(2)}) collective-permute-start(bf16[2,2,256,128]{3,2,1,0:T(8,128)(2,1)} %get-tuple-element.36), channel_id=1, source_target_pairs={{0,2},{2,0},{4,6},{6,4},{8,10},{10,8},{12,14},{14,12},{16,18},{18,... | collective-permute-start | bytes 786440 | tf_op jit(solution)/shard_map/ppermute | solution.py:307
  72.5 12.3 %collective-permute-start.18 = (bf16[2,2,256,128]{3,2,1,0:T(8,128)(2,1)}, bf16[2,2,256,128]{3,2,1,0:T(8,128)(2,1)S(1)}, u32[]{:S(2)}, u32[]{:S(2)}) collective-permute-start(bf16[2,2,256,128]{3,2,1,0:T(8,128)(2,1)} %get-tuple-element.37), channel_id=1, source_target_pairs={{0,4},{2,6},{4,0},{6,2},{8,12},{10,14},{12,8},{14,10},{16,20},{18,... | collective-permute-start | bytes 786440 | tf_op jit(solution)/shard_map/ppermute | solution.py:307
  75.3 9.6 %collective-permute-start.20 = (bf16[1,2,256,128]{3,2,1,0:T(8,128)(2,1)}, bf16[1,2,256,128]{3,2,1,0:T(8,128)(2,1)S(1)}, u32[]{:S(2)}, u32[]{:S(2)}) collective-permute-start(bf16[1,2,256,128]{3,2,1,0:T(8,128)(2,1)} %get-tuple-element.39), channel_id=1, source_target_pairs={{0,6},{2,4},{4,2},{6,0},{8,14},{10,12},{12,10},{14,8},{16,22},{18,... | collective-permute-start | bytes 393224 | tf_op jit(solution)/shard_map/ppermute | solution.py:307
  76.7 9.7 %collective-permute-start.21 = (bf16[1,2,256,128]{3,2,1,0:T(8,128)(2,1)}, bf16[1,2,256,128]{3,2,1,0:T(8,128)(2,1)S(1)}, u32[]{:S(2)}, u32[]{:S(2)}) collective-permute-start(bf16[1,2,256,128]{3,2,1,0:T(8,128)(2,1)} %get-tuple-element.40), channel_id=1, source_target_pairs={{0,2},{2,0},{4,6},{6,4},{8,10},{10,8},{12,14},{14,12},{16,18},{18,... | collective-permute-start | bytes 393224 | tf_op jit(solution)/shard_map/ppermute | solution.py:307
  77.6 9.2 %collective-permute-start.22 = (bf16[1,2,256,128]{3,2,1,0:T(8,128)(2,1)}, bf16[1,2,256,128]{3,2,1,0:T(8,128)(2,1)}, u32[]{:S(2)}, u32[]{:S(2)}) collective-permute-start(bf16[1,2,256,128]{3,2,1,0:T(8,128)(2,1)} %get-tuple-element.41), channel_id=1, source_target_pairs={{0,4},{2,6},{4,0},{6,2},{8,12},{10,14},{12,8},{14,10},{16,20},{18,... | collective-permute-start | bytes 393224 | tf_op jit(solution)/shard_map/ppermute | solution.py:307
  (8 other events, 40.8 us)
where the time goes:
time: 95.1 us; the launch traced here: 93.7 us
  starting transfers between devices  31.9 us (34%)
  waiting for transfers between devices  26 us (27%)
  Pallas kernels  19.7 us (21%)
  blocking collectives  13.1 us (14%)
  local copies, waits for them, and re-layouts  1.92 us (2%)
    ppermute x21, starting transfers between devices, to_member(): return lax.ppermute(array, 'node', [(n, n ^ step) for n in range(nodes)])  26.5 us
    ppermute x21, waiting for transfers between devices, to_member(): return lax.ppermute(array, 'node', [(n, n ^ step) for n in range(nodes)])  19.8 us
    all_to_all x1, blocking collectives, exchange(): lax.all_to_all(array, 'node', split_axis=0, concat_axis=0, tiled=True, ax...  8.75 us
    pallas_call x4, Pallas kernels, pack(): pl.pallas_call(functools.partial(pack_kernel, cubes, tuple(held), message...  7.01 us
    pallas_call x2, Pallas kernels, aggregate(): pl.pallas_call(functools.partial(aggregate_kernel, cubes, limit, messages...  6.83 us
    ppermute x2, waiting for transfers between devices, gather_sums(): lax.ppermute(feat_t, 'node', [(n, (n - unit * GROUP) % nodes) for n in ra...  6.13 us
    ppermute x2, starting transfers between devices, gather_sums(): lax.ppermute(feat_t, 'node', [(n, (n - unit * GROUP) % nodes) for n in ra...  5.42 us
    all_gather x2, blocking collectives, gather_sums(): return lax.all_gather(local, 'col', axis=0, tiled=True)  4.36 us
  transfers between devices with their start and end apart: 23, of which 11 were waited for; matrix products, arithmetic and copies ran while one was open for 0% of the time, Pallas kernels for 10%

commit v1 on v0

--- a/solution.py
+++ b/solution.py
@@ -326,7 +326,8 @@
             array = {at: held[at] for at in sources}
             sent = pack(cubes, words, array, batch, False, work)
             for one, (step, _) in zip(sent, batch):
-                messages.append((step, sources, number == 0 or step == 0))
+                far = number == 0 or step == 0 or (number, step) == (2, 2)
+                messages.append((step, sources, far))
                 received.append(to_member(one, step) if step else one)
     else:
         near = {(0, step): to_member(feat_t, step) if step else feat_t for step in NEAR}
@@ -335,9 +336,11 @@
             (step, ([(0, PASSED[step])] if step in PASSED else []) + list(relayed))
             for step in STEPS
         ]
-        sent = pack(cubes, words, held, batch, True, 0)
+        sent = list(pack(cubes, words, held, batch, True, 0))
+        kept = keep(cubes, words, held)
+        sent[4], kept, lists = lax.optimization_barrier((sent[4], kept, lists))
         received = [to_member(one, step) for one, (step, _) in zip(sent, batch)]
-        received.append(keep(cubes, words, held))
+        received.append(kept)
         messages = [(*one, False) for one in batch] + [(0, list(held), False)]
     local = aggregate(
         cubes, messages, not by_planes, lists, adj_tiles, received, feat_t.shape[1]

time: 95.1 us -> 93.9 us (0.987)
  starting transfers between devices: 31.9 us -> 30.2 us
  waiting for transfers between devices: 26 us -> 27.4 us
    ppermute x21, starting transfers between devices: 26.5 us -> 24.3 us  [to_member(): return lax.ppermute(array, 'node', [(n, n ^ step) for n in range(nodes)])]
    ppermute x21, waiting for transfers between devices: 19.8 us -> 21.1 us  [to_member(): return lax.ppermute(array, 'node', [(n, n ^ step) for n in range(nodes)])]
where the time goes in v1:
time: 93.9 us; the launch traced here: 92.6 us
  starting transfers between devices  30.2 us (32%)
  waiting for transfers between devices  27.4 us (29%)
  Pallas kernels  18.9 us (20%)
  blocking collectives  13.1 us (14%)
  local copies, waits for them, and re-layouts  1.92 us (2%)
    ppermute x21, starting transfers between devices, to_member(): return lax.ppermute(array, 'node', [(n, n ^ step) for n in range(nodes)])  24.3 us
    ppermute x21, waiting for transfers between devices, to_member(): return lax.ppermute(array, 'node', [(n, n ^ step) for n in range(nodes)])  21.1 us
    all_to_all x1, blocking collectives, exchange(): lax.all_to_all(array, 'node', split_axis=0, concat_axis=0, tiled=True, ax...  8.75 us
    pallas_call x4, Pallas kernels, pack(): pl.pallas_call(functools.partial(pack_kernel, cubes, tuple(held), message...  7.01 us
    ppermute x2, waiting for transfers between devices, gather_sums(): lax.ppermute(feat_t, 'node', [(n, (n - unit * GROUP) % nodes) for n in ra...  6.27 us
    pallas_call x2, Pallas kernels, aggregate(): pl.pallas_call(functools.partial(aggregate_kernel, cubes, limit, messages...  5.96 us
    ppermute x2, starting transfers between devices, gather_sums(): lax.ppermute(feat_t, 'node', [(n, (n - unit * GROUP) % nodes) for n in ra...  5.86 us
    all_gather x2, blocking collectives, gather_sums(): return lax.all_gather(local, 'col', axis=0, tiled=True)  4.36 us
  transfers between devices with their start and end apart: 23, of which 11 were waited for; matrix products, arithmetic and copies ran while one was open for 0% of the time, Pallas kernels for 10%

profile of v1, /device:TPU:0, one launch (start us, length us, event | category | flops | bytes accessed | tf_op | source)
XLA Modules:
  0.0 92.6 jit_solution(14894353462807256014)
XLA Ops:
  0.0 4.0 %collective-permute-start = (bf16[256,512]{1,0:T(8,128)(2,1)}, bf16[256,512]{1,0:T(8,128)(2,1)S(1)}, u32[]{:S(2)}, u32[]{:S(2)}) collective-permute-start(bf16[256,512]{1,0:T(8,128)(2,1)} %refs_1_.3), channel_id=1, source_target_pairs={{0,16},{2,18},{4,20},{6,22},{8,24},{10,26},{12,28},{14,30},{16,0},... | collective-permute-start | bytes 786440 | tf_op jit(solution)/shard_map/ppermute | solution.py:310
  7.1 1.6 %collective-permute-start.3 = (bf16[256,512]{1,0:T(8,128)(2,1)}, bf16[256,512]{1,0:T(8,128)(2,1)S(1)}, u32[]{:S(2)}, u32[]{:S(2)}) collective-permute-start(bf16[256,512]{1,0:T(8,128)(2,1)} %refs_1_.3), channel_id=1, source_target_pairs={{0,8},{2,10},{4,12},{6,14},{8,0},{10,2},{12,4},{14,6},{16,24},{18,... | collective-permute-start | bytes 786440 | tf_op jit(solution)/shard_map/ppermute | solution.py:307
  9.3 1.5 %shard_map.91.words_ref = s32[8,2]{1,0:T(8,128)} custom-call(s32[1]{0:T(128)S(6)} %copy.38.count_ref, s32[64]{0:T(128)} %cols_ref.3), custom_call_target="tpu_custom_call" | custom-call | tf_op jit(solution)/shard_map/pallas_call | solution.py:121
  10.8 8.7 %all_to_all.11 = s32[8,1,2]{2,1,0:T(1,128)S(1)} all-to-all(s32[8,1,2]{2,1,0:T(1,128)} %bitcast.9), channel_id=1, replica_groups={{0,2,4,6,8,10,12,14},{16,18,20,22,24,26,28,30},{1,3,5,7,9,11,13,15},{17..., dimensions={0} | all-to-all | bytes 128 | tf_op jit(solution)/shard_map/all_to_all | solution.py:140
  19.8 2.4 %shard_map.93 = (bf16[2,2,256,128]{3,2,1,0:T(8,128)(2,1)}, bf16[1,2,256,128]{3,2,1,0:T(8,128)(2,1)}, bf16[1,2,256,128]{3,2,1,0:T(8,128)(2,1)}, bf16[2,2,256,128]...) custom-call(s32[8,2]{1,0:T(8,128)S(1)} %copy.31.words_ref, ...), custom_call_target="tpu_custom_call" | custom-call | tf_op jit(solution)/shard_map/pallas_call | solution.py:188
  22.8 2.6 %collective-permute-start.4 = (bf16[2,2,256,128]{3,2,1,0:T(8,128)(2,1)}, bf16[2,2,256,128]{3,2,1,0:T(8,128)(2,1)S(1)}, u32[]{:S(2)}, u32[]{:S(2)}) collective-permute-start(bf16[2,2,256,128]{3,2,1,0:T(8,128)(2,1)} %get-tuple-element.29), channel_id=1, source_target_pairs={{0,14},{2,12},{4,10},{6,8},{8,6},{10,4},{12,2},{14,0},{16,30},{18,... | collective-permute-start | bytes 786440 | tf_op jit(solution)/shard_map/ppermute | solution.py:307
  28.3 2.3 %collective-permute-done.5.refs_1_ = bf16[1,2,256,128]{3,2,1,0:T(8,128)(2,1)S(1)} collective-permute-done((bf16[1,2,256,128]{3,2,1,0:T(8,128)(2,1)}, bf16[1,2,256,128]{3,2,1,0:T(8,128)(2,1)S(1)}, u32[]{:S(2)}, u32[]{:S(2)}) %collective-permute-start.5) | collective-permute-done | bytes 131104 | tf_op jit(solution)/shard_map/ppermute | solution.py:307
  31.4 2.5 %shard_map.92.lists_hbm = s32[181]{0:T(256)} custom-call(s32[1]{0:T(128)S(6)} %copy.38.count_ref, s32[64]{0:T(128)} %rows_ref.1, s32[64]{0:T(128)} %cols_ref.3, s32[8,2]{1,0:T(8,128)} %shard_map.91.words_ref), custom_call_target="tpu_custom_call" | custom-call | tf_op jit(solution)/shard_map/pallas_call | solution.py:127
  37.8 4.8 %collective-permute-done.8.refs_4_ = bf16[1,2,256,128]{3,2,1,0:T(8,128)(2,1)S(1)} collective-permute-done((bf16[1,2,256,128]{3,2,1,0:T(8,128)(2,1)}, bf16[1,2,256,128]{3,2,1,0:T(8,128)(2,1)S(1)}, u32[]{:S(2)}, u32[]{:S(2)}) %collective-permute-start.8) | collective-permute-done | bytes 131104 | tf_op jit(solution)/shard_map/ppermute | solution.py:307
  43.8 3.1 %shard_map.95 = bf16[256,512]{1,0:T(8,128)(2,1)S(1)} custom-call(s32[181]{0:T(256)} %shard_map.92.lists_hbm, bf16[64,128,128]{2,1,0:T(8,128)(2,1)} %tiles.3, bf16[2,2,256,128]{3,2,1,0:T(8,128)(2,1)S(1)} %collective-permute-done.4.refs_0_, bf16[1,2,256,128]{3,2,1,0:T(8,128)(2,1)S(1)} %collective-permute-done.5.refs_1_, ...), custom_call_target="tpu_custom_call" | custom-call | flops 536870912 | bytes 4194304 | tf_op jit(solution)/shard_map/pallas_call | solution.py:287
  46.9 2.2 %all_gather.6 = bf16[512,512]{1,0:T(8,128)(2,1)S(1)} all-gather(bf16[256,512]{1,0:T(8,128)(2,1)S(1)} %shard_map.95), channel_id=1, replica_groups=mesh['node'=16,'col'=2] {'col'}, dimensions={0}, use_global_device_ids=true | all-gather | bytes 786432 | tf_op jit(solution)/shard_map/all_gather | solution.py:348
  49.4 1.8 %collective-permute-start.15 = (bf16[256,512]{1,0:T(8,128)(2,1)S(1)}, bf16[256,512]{1,0:T(8,128)(2,1)S(1)}, u32[]{:S(2)}, u32[]{:S(2)}) collective-permute-start(bf16[256,512]{1,0:T(8,128)(2,1)S(1)} %fusion.2.refs_0_), channel_id=1, source_target_pairs={{0,16},{2,18},{4,20},{6,22},{8,24},{10,26},{12,28},{14,30},{16,0},... | collective-permute-start | bytes 786440 | tf_op jit(solution)/shard_map/ppermute | solution.py:310
  51.2 1.9 %collective-permute-start.14 = (bf16[256,512]{1,0:T(8,128)(2,1)S(1)}, bf16[256,512]{1,0:T(8,128)(2,1)S(1)}, u32[]{:S(2)}, u32[]{:S(2)}) collective-permute-start(bf16[256,512]{1,0:T(8,128)(2,1)S(1)} %fusion.2.refs_0_), channel_id=1, source_target_pairs={{0,8},{2,10},{4,12},{6,14},{8,0},{10,2},{12,4},{14,6},{16,24},{18,... | collective-permute-start | bytes 786440 | tf_op jit(solution)/shard_map/ppermute | solution.py:307
  55.1 2.0 %collective-permute-start.12 = (bf16[1,2,256,128]{3,2,1,0:T(8,128)(2,1)}, bf16[1,2,256,128]{3,2,1,0:T(8,128)(2,1)S(1)}, u32[]{:S(2)}, u32[]{:S(2)}) collective-permute-start(bf16[1,2,256,128]{3,2,1,0:T(8,128)(2,1)} %get-tuple-element.38), channel_id=1, source_target_pairs={{0,2},{2,0},{4,6},{6,4},{8,10},{10,8},{12,14},{14,12},{16,18},{18,... | collective-permute-start | bytes 393224 | tf_op jit(solution)/shard_map/ppermute | solution.py:307
  58.1 6.3 %collective-permute-done.15.refs_1_ = bf16[256,512]{1,0:T(8,128)(2,1)S(1)} collective-permute-done((bf16[256,512]{1,0:T(8,128)(2,1)S(1)}, bf16[256,512]{1,0:T(8,128)(2,1)S(1)}, u32[]{:S(2)}, u32[]{:S(2)}) %collective-permute-start.15) | collective-permute-done | bytes 262176 | tf_op jit(solution)/shard_map/ppermute | solution.py:310
  64.5 1.7 %shard_map.97 = (bf16[2,2,256,128]{3,2,1,0:T(8,128)(2,1)}, bf16[2,2,256,128]{3,2,1,0:T(8,128)(2,1)}, bf16[2,2,256,128]{3,2,1,0:T(8,128)(2,1)}, bf16[2,2,256,128]{3,2,1,0:T(8,128)(2,1)}) custom-call(s32[8,2]{1,0:T(8,128)S(1)} %copy.31.words_ref, bf16[256,512]{1,0:T(8,128)(2,1)S(1)} %collective-permute-done.14.refs_0_, ...), custom_call_target="tpu_custom_call" | custom-call | flops 49999998976 | tf_op jit(solution)/shard_map/pallas_call | solution.py:188
  66.2 2.2 %collective-permute-start.16 = (bf16[2,2,256,128]{3,2,1,0:T(8,128)(2,1)}, bf16[2,2,256,128]{3,2,1,0:T(8,128)(2,1)S(1)}, u32[]{:S(2)}, u32[]{:S(2)}) collective-permute-start(bf16[2,2,256,128]{3,2,1,0:T(8,128)(2,1)} %get-tuple-element.41), channel_id=1, source_target_pairs={{0,6},{2,4},{4,2},{6,0},{8,14},{10,12},{12,10},{14,8},{16,22},{18,... | collective-permute-start | bytes 786440 | tf_op jit(solution)/shard_map/ppermute | solution.py:307
  69.1 3.1 %collective-permute-done.19.refs_0_ = bf16[256,512]{1,0:T(8,128)(2,1)S(1)} collective-permute-done((bf16[256,512]{1,0:T(8,128)(2,1)S(1)}, bf16[256,512]{1,0:T(8,128)(2,1)S(1)}, u32[]{:S(2)}, u32[]{:S(2)}) %collective-permute-start.19) | collective-permute-done | bytes 262176 | tf_op jit(solution)/shard_map/ppermute | solution.py:307
  73.7 1.7 %collective-permute-start.20 = (bf16[1,2,256,128]{3,2,1,0:T(8,128)(2,1)}, bf16[1,2,256,128]{3,2,1,0:T(8,128)(2,1)S(1)}, u32[]{:S(2)}, u32[]{:S(2)}) collective-permute-start(bf16[1,2,256,128]{3,2,1,0:T(8,128)(2,1)} %get-tuple-element.45), channel_id=1, source_target_pairs={{0,6},{2,4},{4,2},{6,0},{8,14},{10,12},{12,10},{14,8},{16,22},{18,... | collective-permute-start | bytes 393224 | tf_op jit(solution)/shard_map/ppermute | solution.py:307
  75.4 1.9 %collective-permute-start.21 = (bf16[1,2,256,128]{3,2,1,0:T(8,128)(2,1)}, bf16[1,2,256,128]{3,2,1,0:T(8,128)(2,1)S(1)}, u32[]{:S(2)}, u32[]{:S(2)}) collective-permute-start(bf16[1,2,256,128]{3,2,1,0:T(8,128)(2,1)} %get-tuple-element.46), channel_id=1, source_target_pairs={{0,2},{2,0},{4,6},{6,4},{8,10},{10,8},{12,14},{14,12},{16,18},{18,... | collective-permute-start | bytes 393224 | tf_op jit(solution)/shard_map/ppermute | solution.py:307
  77.5 3.6 %collective-permute-done.17.refs_5_ = bf16[2,2,256,128]{3,2,1,0:T(8,128)(2,1)S(1)} collective-permute-done((bf16[2,2,256,128]{3,2,1,0:T(8,128)(2,1)}, bf16[2,2,256,128]{3,2,1,0:T(8,128)(2,1)S(1)}, u32[]{:S(2)}, u32[]{:S(2)}) %collective-permute-start.17) | collective-permute-done | bytes 262176 | tf_op jit(solution)/shard_map/ppermute | solution.py:307
  81.1 3.4 %collective-permute-done.18.refs_6_ = bf16[2,2,256,128]{3,2,1,0:T(8,128)(2,1)S(1)} collective-permute-done((bf16[2,2,256,128]{3,2,1,0:T(8,128)(2,1)}, bf16[2,2,256,128]{3,2,1,0:T(8,128)(2,1)S(1)}, u32[]{:S(2)}, u32[]{:S(2)}) %collective-permute-start.18) | collective-permute-done | bytes 262176 | tf_op jit(solution)/shard_map/ppermute | solution.py:307
  86.4 2.8 %shard_map.99 = bf16[256,512]{1,0:T(8,128)(2,1)S(1)} custom-call(s32[181]{0:T(256)} %shard_map.92.lists_hbm, bf16[64,128,128]{2,1,0:T(8,128)(2,1)S(1)} %copy-done.1, bf16[1,2,256,128]{3,2,1,0:T(8,128)(2,1)} %copy-done.4, bf16[1,2,256,128]{3,2,1,0:T(8,128)(2,1)} %copy-done.5, bf16[1,2,256,128]{3,2,1,0:T(8,128)(2,1)} %copy-done.6, ...), custom_call_target="tpu_custom_call" | custom-call | flops 536870912 | bytes 4194304 | tf_op jit(solution)/shard_map/pallas_call | solution.py:287
  89.3 2.2 %all_gather.7.aggregated = bf16[512,512]{1,0:T(8,128)(2,1)S(1)} all-gather(bf16[256,512]{1,0:T(8,128)(2,1)S(1)} %shard_map.99), channel_id=1, replica_groups=mesh['node'=16,'col'=2] {'col'}, dimensions={0}, use_global_device_ids=true | all-gather | bytes 786432 | tf_op jit(solution)/shard_map/all_gather | solution.py:348
  (57 shorter events, 21.4 us)
Async XLA Ops:
  0.0 49.1 %copy-start = (bf16[256,512]{1,0:T(8,128)(2,1)S(1)}, bf16[256,512]{1,0:T(8,128)(2,1)}, u32[]{:S(2)}) copy-start(bf16[256,512]{1,0:T(8,128)(2,1)} %param.14) | copy-start | bytes 786436
  0.0 19.7 %collective-permute-start = (bf16[256,512]{1,0:T(8,128)(2,1)}, bf16[256,512]{1,0:T(8,128)(2,1)S(1)}, u32[]{:S(2)}, u32[]{:S(2)}) collective-permute-start(bf16[256,512]{1,0:T(8,128)(2,1)} %refs_1_.3), channel_id=1, source_target_pairs={{0,16},{2,18},{4,20},{6,22},{8,24},{10,26},{12,28},{14,30},{16,0},... | collective-permute-start | bytes 786440 | tf_op jit(solution)/shard_map/ppermute | solution.py:310
  4.0 15.7 %collective-permute-start.1 = (bf16[256,512]{1,0:T(8,128)(2,1)}, bf16[256,512]{1,0:T(8,128)(2,1)S(1)}, u32[]{:S(2)}, u32[]{:S(2)}) collective-permute-start(bf16[256,512]{1,0:T(8,128)(2,1)} %refs_1_.3), channel_id=1, source_target_pairs={{0,2},{2,0},{4,6},{6,4},{8,10},{10,8},{12,14},{14,12},{16,18},{18,... | collective-permute-start | bytes 786440 | tf_op jit(solution)/shard_map/ppermute | solution.py:307
  5.5 14.2 %collective-permute-start.2 = (bf16[256,512]{1,0:T(8,128)(2,1)}, bf16[256,512]{1,0:T(8,128)(2,1)S(1)}, u32[]{:S(2)}, u32[]{:S(2)}) collective-permute-start(bf16[256,512]{1,0:T(8,128)(2,1)} %refs_1_.3), channel_id=1, source_target_pairs={{0,4},{2,6},{4,0},{6,2},{8,12},{10,14},{12,8},{14,10},{16,20},{18,... | collective-permute-start | bytes 786440 | tf_op jit(solution)/shard_map/ppermute | solution.py:307
  7.1 12.7 %collective-permute-start.3 = (bf16[256,512]{1,0:T(8,128)(2,1)}, bf16[256,512]{1,0:T(8,128)(2,1)S(1)}, u32[]{:S(2)}, u32[]{:S(2)}) collective-permute-start(bf16[256,512]{1,0:T(8,128)(2,1)} %refs_1_.3), channel_id=1, source_target_pairs={{0,8},{2,10},{4,12},{6,14},{8,0},{10,2},{12,4},{14,6},{16,24},{18,... | collective-permute-start | bytes 786440 | tf_op jit(solution)/shard_map/ppermute | solution.py:307
  22.1 8.5 %collective-permute-start.5 = (bf16[1,2,256,128]{3,2,1,0:T(8,128)(2,1)}, bf16[1,2,256,128]{3,2,1,0:T(8,128)(2,1)S(1)}, u32[]{:S(2)}, u32[]{:S(2)}) collective-permute-start(bf16[1,2,256,128]{3,2,1,0:T(8,128)(2,1)} %get-tuple-element.30), channel_id=1, source_target_pairs={{0,12},{2,14},{4,8},{6,10},{8,4},{10,6},{12,0},{14,2},{16,28},{18,... | collective-permute-start | bytes 393224 | tf_op jit(solution)/shard_map/ppermute | solution.py:307
  22.8 19.8 %collective-permute-start.4 = (bf16[2,2,256,128]{3,2,1,0:T(8,128)(2,1)}, bf16[2,2,256,128]{3,2,1,0:T(8,128)(2,1)S(1)}, u32[]{:S(2)}, u32[]{:S(2)}) collective-permute-start(bf16[2,2,256,128]{3,2,1,0:T(8,128)(2,1)} %get-tuple-element.29), channel_id=1, source_target_pairs={{0,14},{2,12},{4,10},{6,8},{8,6},{10,4},{12,2},{14,0},{16,30},{18,... | collective-permute-start | bytes 786440 | tf_op jit(solution)/shard_map/ppermute | solution.py:307
  25.4 11.0 %collective-permute-start.6 = (bf16[1,2,256,128]{3,2,1,0:T(8,128)(2,1)}, bf16[1,2,256,128]{3,2,1,0:T(8,128)(2,1)S(1)}, u32[]{:S(2)}, u32[]{:S(2)}) collective-permute-start(bf16[1,2,256,128]{3,2,1,0:T(8,128)(2,1)} %get-tuple-element.31), channel_id=1, source_target_pairs={{0,6},{2,4},{4,2},{6,0},{8,14},{10,12},{12,10},{14,8},{16,22},{18,... | collective-permute-start | bytes 393224 | tf_op jit(solution)/shard_map/ppermute | solution.py:307
  26.9 15.7 %collective-permute-start.7 = (bf16[2,2,256,128]{3,2,1,0:T(8,128)(2,1)}, bf16[2,2,256,128]{3,2,1,0:T(8,128)(2,1)S(1)}, u32[]{:S(2)}, u32[]{:S(2)}) collective-permute-start(bf16[2,2,256,128]{3,2,1,0:T(8,128)(2,1)} %get-tuple-element.32), channel_id=1, source_target_pairs={{0,8},{2,10},{4,12},{6,14},{8,0},{10,2},{12,4},{14,6},{16,24},{18,... | collective-permute-start | bytes 786440 | tf_op jit(solution)/shard_map/ppermute | solution.py:307
  27.1 16.6 %collective-permute-start.9 = (bf16[2,2,256,128]{3,2,1,0:T(8,128)(2,1)}, bf16[2,2,256,128]{3,2,1,0:T(8,128)(2,1)S(1)}, u32[]{:S(2)}, u32[]{:S(2)}) collective-permute-start(bf16[2,2,256,128]{3,2,1,0:T(8,128)(2,1)} %get-tuple-element.34), channel_id=1, source_target_pairs={{0,2},{2,0},{4,6},{6,4},{8,10},{10,8},{12,14},{14,12},{16,18},{18,... | collective-permute-start | bytes 786440 | tf_op jit(solution)/shard_map/ppermute | solution.py:307
  30.6 13.1 %collective-permute-start.10 = (bf16[2,2,256,128]{3,2,1,0:T(8,128)(2,1)}, bf16[2,2,256,128]{3,2,1,0:T(8,128)(2,1)S(1)}, u32[]{:S(2)}, u32[]{:S(2)}) collective-permute-start(bf16[2,2,256,128]{3,2,1,0:T(8,128)(2,1)} %get-tuple-element.35), channel_id=1, source_target_pairs={{0,4},{2,6},{4,0},{6,2},{8,12},{10,14},{12,8},{14,10},{16,20},{18,... | collective-permute-start | bytes 786440 | tf_op jit(solution)/shard_map/ppermute | solution.py:307
  36.4 6.2 %collective-permute-start.8 = (bf16[1,2,256,128]{3,2,1,0:T(8,128)(2,1)}, bf16[1,2,256,128]{3,2,1,0:T(8,128)(2,1)S(1)}, u32[]{:S(2)}, u32[]{:S(2)}) collective-permute-start(bf16[1,2,256,128]{3,2,1,0:T(8,128)(2,1)} %get-tuple-element.33), channel_id=1, source_target_pairs={{0,10},{2,8},{4,14},{6,12},{8,2},{10,0},{12,6},{14,4},{16,26},{18,... | collective-permute-start | bytes 393224 | tf_op jit(solution)/shard_map/ppermute | solution.py:307
  49.4 15.0 %collective-permute-start.15 = (bf16[256,512]{1,0:T(8,128)(2,1)S(1)}, bf16[256,512]{1,0:T(8,128)(2,1)S(1)}, u32[]{:S(2)}, u32[]{:S(2)}) collective-permute-start(bf16[256,512]{1,0:T(8,128)(2,1)S(1)} %fusion.2.refs_0_), channel_id=1, source_target_pairs={{0,16},{2,18},{4,20},{6,22},{8,24},{10,26},{12,28},{14,30},{16,0},... | collective-permute-start | bytes 786440 | tf_op jit(solution)/shard_map/ppermute | solution.py:310
  51.2 13.3 %collective-permute-start.14 = (bf16[256,512]{1,0:T(8,128)(2,1)S(1)}, bf16[256,512]{1,0:T(8,128)(2,1)S(1)}, u32[]{:S(2)}, u32[]{:S(2)}) collective-permute-start(bf16[256,512]{1,0:T(8,128)(2,1)S(1)} %fusion.2.refs_0_), channel_id=1, source_target_pairs={{0,8},{2,10},{4,12},{6,14},{8,0},{10,2},{12,4},{14,6},{16,24},{18,... | collective-permute-start | bytes 786440 | tf_op jit(solution)/shard_map/ppermute | solution.py:307
  54.6 13.8 %collective-permute-start.11 = (bf16[1,2,256,128]{3,2,1,0:T(8,128)(2,1)}, bf16[1,2,256,128]{3,2,1,0:T(8,128)(2,1)S(1)}, u32[]{:S(2)}, u32[]{:S(2)}) collective-permute-start(bf16[1,2,256,128]{3,2,1,0:T(8,128)(2,1)} %get-tuple-element.37), channel_id=1, source_target_pairs={{0,6},{2,4},{4,2},{6,0},{8,14},{10,12},{12,10},{14,8},{16,22},{18,... | collective-permute-start | bytes 393224 | tf_op jit(solution)/shard_map/ppermute | solution.py:307
  55.1 18.5 %collective-permute-start.12 = (bf16[1,2,256,128]{3,2,1,0:T(8,128)(2,1)}, bf16[1,2,256,128]{3,2,1,0:T(8,128)(2,1)S(1)}, u32[]{:S(2)}, u32[]{:S(2)}) collective-permute-start(bf16[1,2,256,128]{3,2,1,0:T(8,128)(2,1)} %get-tuple-element.38), channel_id=1, source_target_pairs={{0,2},{2,0},{4,6},{6,4},{8,10},{10,8},{12,14},{14,12},{16,18},{18,... | collective-permute-start | bytes 393224 | tf_op jit(solution)/shard_map/ppermute | solution.py:307
  57.2 18.2 %collective-permute-start.13 = (bf16[1,2,256,128]{3,2,1,0:T(8,128)(2,1)}, bf16[1,2,256,128]{3,2,1,0:T(8,128)(2,1)S(1)}, u32[]{:S(2)}, u32[]{:S(2)}) collective-permute-start(bf16[1,2,256,128]{3,2,1,0:T(8,128)(2,1)} %get-tuple-element.39), channel_id=1, source_target_pairs={{0,4},{2,6},{4,0},{6,2},{8,12},{10,14},{12,8},{14,10},{16,20},{18,... | collective-permute-start | bytes 393224 | tf_op jit(solution)/shard_map/ppermute | solution.py:307
  64.4 7.7 %collective-permute-start.19 = (bf16[256,512]{1,0:T(8,128)(2,1)S(1)}, bf16[256,512]{1,0:T(8,128)(2,1)S(1)}, u32[]{:S(2)}, u32[]{:S(2)}) collective-permute-start(bf16[256,512]{1,0:T(8,128)(2,1)S(1)} %collective-permute-done.15.refs_1_), channel_id=1, source_target_pairs={{0,8},{2,10},{4,12},{6,14},{8,0},{10,2},{12,4},{14,6},{16,24},{18,... | collective-permute-start | bytes 786440 | tf_op jit(solution)/shard_map/ppermute | solution.py:307
  66.2 11.1 %collective-permute-start.16 = (bf16[2,2,256,128]{3,2,1,0:T(8,128)(2,1)}, bf16[2,2,256,128]{3,2,1,0:T(8,128)(2,1)S(1)}, u32[]{:S(2)}, u32[]{:S(2)}) collective-permute-start(bf16[2,2,256,128]{3,2,1,0:T(8,128)(2,1)} %get-tuple-element.41), channel_id=1, source_target_pairs={{0,6},{2,4},{4,2},{6,0},{8,14},{10,12},{12,10},{14,8},{16,22},{18,... | collective-permute-start | bytes 786440 | tf_op jit(solution)/shard_map/ppermute | solution.py:307
  69.0 12.0 %collective-permute-start.17 = (bf16[2,2,256,128]{3,2,1,0:T(8,128)(2,1)}, bf16[2,2,256,128]{3,2,1,0:T(8,128)(2,1)S(1)}, u32[]{:S(2)}, u32[]{:S(2)}) collective-permute-start(bf16[2,2,256,128]{3,2,1,0:T(8,128)(2,1)} %get-tuple-element.42), channel_id=1, source_target_pairs={{0,2},{2,0},{4,6},{6,4},{8,10},{10,8},{12,14},{14,12},{16,18},{18,... | collective-permute-start | bytes 786440 | tf_op jit(solution)/shard_map/ppermute | solution.py:307
  72.2 12.3 %collective-permute-start.18 = (bf16[2,2,256,128]{3,2,1,0:T(8,128)(2,1)}, bf16[2,2,256,128]{3,2,1,0:T(8,128)(2,1)S(1)}, u32[]{:S(2)}, u32[]{:S(2)}) collective-permute-start(bf16[2,2,256,128]{3,2,1,0:T(8,128)(2,1)} %get-tuple-element.43), channel_id=1, source_target_pairs={{0,4},{2,6},{4,0},{6,2},{8,12},{10,14},{12,8},{14,10},{16,20},{18,... | collective-permute-start | bytes 786440 | tf_op jit(solution)/shard_map/ppermute | solution.py:307
  73.7 11.3 %collective-permute-start.20 = (bf16[1,2,256,128]{3,2,1,0:T(8,128)(2,1)}, bf16[1,2,256,128]{3,2,1,0:T(8,128)(2,1)S(1)}, u32[]{:S(2)}, u32[]{:S(2)}) collective-permute-start(bf16[1,2,256,128]{3,2,1,0:T(8,128)(2,1)} %get-tuple-element.45), channel_id=1, source_target_pairs={{0,6},{2,4},{4,2},{6,0},{8,14},{10,12},{12,10},{14,8},{16,22},{18,... | collective-permute-start | bytes 393224 | tf_op jit(solution)/shard_map/ppermute | solution.py:307
  75.4 9.6 %collective-permute-start.21 = (bf16[1,2,256,128]{3,2,1,0:T(8,128)(2,1)}, bf16[1,2,256,128]{3,2,1,0:T(8,128)(2,1)S(1)}, u32[]{:S(2)}, u32[]{:S(2)}) collective-permute-start(bf16[1,2,256,128]{3,2,1,0:T(8,128)(2,1)} %get-tuple-element.46), channel_id=1, source_target_pairs={{0,2},{2,0},{4,6},{6,4},{8,10},{10,8},{12,14},{14,12},{16,18},{18,... | collective-permute-start | bytes 393224 | tf_op jit(solution)/shard_map/ppermute | solution.py:307
  77.2 9.2 %collective-permute-start.22 = (bf16[1,2,256,128]{3,2,1,0:T(8,128)(2,1)}, bf16[1,2,256,128]{3,2,1,0:T(8,128)(2,1)}, u32[]{:S(2)}, u32[]{:S(2)}) collective-permute-start(bf16[1,2,256,128]{3,2,1,0:T(8,128)(2,1)} %get-tuple-element.47), channel_id=1, source_target_pairs={{0,4},{2,6},{4,0},{6,2},{8,12},{10,14},{12,8},{14,10},{16,20},{18,... | collective-permute-start | bytes 393224 | tf_op jit(solution)/shard_map/ppermute | solution.py:307
  (8 other events, 45.3 us)

commit v2 on v1

--- a/solution.py
+++ b/solution.py
@@ -12,7 +12,7 @@
 GROUP = 8
 NEAR = (0, 1, 2, 4)
 PASSED = {7: 0, 4: 1, 1: 2, 2: 4}
-STEPS = (7, 6, 3, 4, 5, 1, 2)
+STEPS = (7, 6, 5, 4, 3, 1, 2)
 DEPTH = 4
 RELAY_WORK = 50_000_000_000
 WIDTH = 4

time: 93.9 us -> 93.4 us (level)
  starting transfers between devices: 30.2 us -> 34.1 us
  waiting for transfers between devices: 27.4 us -> 25.3 us
  Pallas kernels: 18.9 us -> 17.5 us
    ppermute x21, starting transfers between devices: 24.3 us -> 27.9 us  [to_member(): return lax.ppermute(array, 'node', [(n, n ^ step) for n in range(nodes)])]
    ppermute x21, waiting for transfers between devices: 21.1 us -> 18.8 us  [to_member(): return lax.ppermute(array, 'node', [(n, n ^ step) for n in range(nodes)])]
  transfers between devices with their start and end apart: 23 -> 23, of which waited for: 11 -> 10; matrix products, arithmetic and copies ran while one was open for 0% -> 0% of each run, Pallas kernels for 10% -> 10%
where the time goes in v2:
time: 93.4 us; the launch traced here: 93 us
  starting transfers between devices  34.1 us (37%)
  waiting for transfers between devices  25.3 us (27%)
  Pallas kernels  17.5 us (19%)
  blocking collectives  13.1 us (14%)
  local copies, waits for them, and re-layouts  1.92 us (2%)
    ppermute x21, starting transfers between devices, to_member(): return lax.ppermute(array, 'node', [(n, n ^ step) for n in range(nodes)])  27.9 us
    ppermute x21, waiting for transfers between devices, to_member(): return lax.ppermute(array, 'node', [(n, n ^ step) for n in range(nodes)])  18.8 us
    all_to_all x1, blocking collectives, exchange(): lax.all_to_all(array, 'node', split_axis=0, concat_axis=0, tiled=True, ax...  8.75 us
    pallas_call x4, Pallas kernels, pack(): pl.pallas_call(functools.partial(pack_kernel, cubes, tuple(held), message...  7 us
    ppermute x2, waiting for transfers between devices, gather_sums(): lax.ppermute(feat_t, 'node', [(n, (n - unit * GROUP) % nodes) for n in ra...  6.46 us
    ppermute x2, starting transfers between devices, gather_sums(): lax.ppermute(feat_t, 'node', [(n, (n - unit * GROUP) % nodes) for n in ra...  6.19 us
    pallas_call x2, Pallas kernels, aggregate(): pl.pallas_call(functools.partial(aggregate_kernel, cubes, limit, messages...  5.08 us
    all_gather x2, blocking collectives, gather_sums(): return lax.all_gather(local, 'col', axis=0, tiled=True)  4.36 us
  transfers between devices with their start and end apart: 23, of which 10 were waited for; matrix products, arithmetic and copies ran while one was open for 0% of the time, Pallas kernels for 10%

profile of v2, /device:TPU:0, one launch (start us, length us, event | category | flops | bytes accessed | tf_op | source)
XLA Modules:
  0.0 93.0 jit_solution(17077683505767084186)
XLA Ops:
  0.0 4.0 %collective-permute-start = (bf16[256,512]{1,0:T(8,128)(2,1)}, bf16[256,512]{1,0:T(8,128)(2,1)S(1)}, u32[]{:S(2)}, u32[]{:S(2)}) collective-permute-start(bf16[256,512]{1,0:T(8,128)(2,1)} %refs_1_.3), channel_id=1, source_target_pairs={{0,16},{2,18},{4,20},{6,22},{8,24},{10,26},{12,28},{14,30},{16,0},... | collective-permute-start | bytes 786440 | tf_op jit(solution)/shard_map/ppermute | solution.py:310
  7.1 1.6 %collective-permute-start.3 = (bf16[256,512]{1,0:T(8,128)(2,1)}, bf16[256,512]{1,0:T(8,128)(2,1)S(1)}, u32[]{:S(2)}, u32[]{:S(2)}) collective-permute-start(bf16[256,512]{1,0:T(8,128)(2,1)} %refs_1_.3), channel_id=1, source_target_pairs={{0,8},{2,10},{4,12},{6,14},{8,0},{10,2},{12,4},{14,6},{16,24},{18,... | collective-permute-start | bytes 786440 | tf_op jit(solution)/shard_map/ppermute | solution.py:307
  9.3 1.5 %shard_map.91.words_ref = s32[8,2]{1,0:T(8,128)} custom-call(s32[1]{0:T(128)S(6)} %copy.38.count_ref, s32[64]{0:T(128)} %cols_ref.3), custom_call_target="tpu_custom_call" | custom-call | tf_op jit(solution)/shard_map/pallas_call | solution.py:121
  10.8 8.7 %all_to_all.11 = s32[8,1,2]{2,1,0:T(1,128)S(1)} all-to-all(s32[8,1,2]{2,1,0:T(1,128)} %bitcast.9), channel_id=1, replica_groups={{0,2,4,6,8,10,12,14},{16,18,20,22,24,26,28,30},{1,3,5,7,9,11,13,15},{17..., dimensions={0} | all-to-all | bytes 128 | tf_op jit(solution)/shard_map/all_to_all | solution.py:140
  19.8 2.4 %shard_map.93 = (bf16[2,2,256,128]{3,2,1,0:T(8,128)(2,1)}, bf16[1,2,256,128]{3,2,1,0:T(8,128)(2,1)}, bf16[1,2,256,128]{3,2,1,0:T(8,128)(2,1)}, bf16[2,2,256,128]...) custom-call(s32[8,2]{1,0:T(8,128)S(1)} %copy.31.words_ref, ...), custom_call_target="tpu_custom_call" | custom-call | tf_op jit(solution)/shard_map/pallas_call | solution.py:188
  22.8 2.6 %collective-permute-start.4 = (bf16[2,2,256,128]{3,2,1,0:T(8,128)(2,1)}, bf16[2,2,256,128]{3,2,1,0:T(8,128)(2,1)S(1)}, u32[]{:S(2)}, u32[]{:S(2)}) collective-permute-start(bf16[2,2,256,128]{3,2,1,0:T(8,128)(2,1)} %get-tuple-element.29), channel_id=1, source_target_pairs={{0,14},{2,12},{4,10},{6,8},{8,6},{10,4},{12,2},{14,0},{16,30},{18,... | collective-permute-start | bytes 786440 | tf_op jit(solution)/shard_map/ppermute | solution.py:307
  31.1 2.0 %shard_map.92.lists_hbm = s32[181]{0:T(256)} custom-call(s32[1]{0:T(128)S(6)} %copy.38.count_ref, s32[64]{0:T(128)} %rows_ref.1, s32[64]{0:T(128)} %cols_ref.3, s32[8,2]{1,0:T(8,128)} %shard_map.91.words_ref), custom_call_target="tpu_custom_call" | custom-call | tf_op jit(solution)/shard_map/pallas_call | solution.py:127
  34.9 3.3 %collective-permute-done.6.refs_2_ = bf16[1,2,256,128]{3,2,1,0:T(8,128)(2,1)S(1)} collective-permute-done((bf16[1,2,256,128]{3,2,1,0:T(8,128)(2,1)}, bf16[1,2,256,128]{3,2,1,0:T(8,128)(2,1)S(1)}, u32[]{:S(2)}, u32[]{:S(2)}) %collective-permute-start.6) | collective-permute-done | bytes 131104 | tf_op jit(solution)/shard_map/ppermute | solution.py:307
  39.7 4.6 %collective-permute-done.8.refs_4_ = bf16[1,2,256,128]{3,2,1,0:T(8,128)(2,1)S(1)} collective-permute-done((bf16[1,2,256,128]{3,2,1,0:T(8,128)(2,1)}, bf16[1,2,256,128]{3,2,1,0:T(8,128)(2,1)S(1)}, u32[]{:S(2)}, u32[]{:S(2)}) %collective-permute-start.8) | collective-permute-done | bytes 131104 | tf_op jit(solution)/shard_map/ppermute | solution.py:307
  44.3 2.7 %shard_map.95 = bf16[256,512]{1,0:T(8,128)(2,1)S(1)} custom-call(s32[181]{0:T(256)} %shard_map.92.lists_hbm, bf16[64,128,128]{2,1,0:T(8,128)(2,1)} %tiles.3, bf16[2,2,256,128]{3,2,1,0:T(8,128)(2,1)S(1)} %collective-permute-done.4.refs_0_, bf16[1,2,256,128]{3,2,1,0:T(8,128)(2,1)S(1)} %collective-permute-done.5.refs_1_, ...), custom_call_target="tpu_custom_call" | custom-call | flops 536870912 | bytes 4194304 | tf_op jit(solution)/shard_map/pallas_call | solution.py:287
  47.0 2.2 %all_gather.6 = bf16[512,512]{1,0:T(8,128)(2,1)S(1)} all-gather(bf16[256,512]{1,0:T(8,128)(2,1)S(1)} %shard_map.95), channel_id=1, replica_groups=mesh['node'=16,'col'=2] {'col'}, dimensions={0}, use_global_device_ids=true | all-gather | bytes 786432 | tf_op jit(solution)/shard_map/all_gather | solution.py:348
  49.5 2.2 %collective-permute-start.15 = (bf16[256,512]{1,0:T(8,128)(2,1)S(1)}, bf16[256,512]{1,0:T(8,128)(2,1)S(1)}, u32[]{:S(2)}, u32[]{:S(2)}) collective-permute-start(bf16[256,512]{1,0:T(8,128)(2,1)S(1)} %fusion.2.refs_0_), channel_id=1, source_target_pairs={{0,16},{2,18},{4,20},{6,22},{8,24},{10,26},{12,28},{14,30},{16,0},... | collective-permute-start | bytes 786440 | tf_op jit(solution)/shard_map/ppermute | solution.py:310
  54.5 2.9 %collective-permute-start.11 = (bf16[1,2,256,128]{3,2,1,0:T(8,128)(2,1)}, bf16[1,2,256,128]{3,2,1,0:T(8,128)(2,1)S(1)}, u32[]{:S(2)}, u32[]{:S(2)}) collective-permute-start(bf16[1,2,256,128]{3,2,1,0:T(8,128)(2,1)} %get-tuple-element.37), channel_id=1, source_target_pairs={{0,6},{2,4},{4,2},{6,0},{8,14},{10,12},{12,10},{14,8},{16,22},{18,... | collective-permute-start | bytes 393224 | tf_op jit(solution)/shard_map/ppermute | solution.py:307
  58.0 6.5 %collective-permute-done.15.refs_1_ = bf16[256,512]{1,0:T(8,128)(2,1)S(1)} collective-permute-done((bf16[256,512]{1,0:T(8,128)(2,1)S(1)}, bf16[256,512]{1,0:T(8,128)(2,1)S(1)}, u32[]{:S(2)}, u32[]{:S(2)}) %collective-permute-start.15) | collective-permute-done | bytes 262176 | tf_op jit(solution)/shard_map/ppermute | solution.py:310
  64.9 1.7 %shard_map.97 = (bf16[2,2,256,128]{3,2,1,0:T(8,128)(2,1)}, bf16[2,2,256,128]{3,2,1,0:T(8,128)(2,1)}, bf16[2,2,256,128]{3,2,1,0:T(8,128)(2,1)}, bf16[2,2,256,128]{3,2,1,0:T(8,128)(2,1)}) custom-call(s32[8,2]{1,0:T(8,128)S(1)} %copy.31.words_ref, bf16[256,512]{1,0:T(8,128)(2,1)S(1)} %collective-permute-done.14.refs_0_, ...), custom_call_target="tpu_custom_call" | custom-call | flops 49999998976 | tf_op jit(solution)/shard_map/pallas_call | solution.py:188
  68.5 2.0 %collective-permute-start.17 = (bf16[2,2,256,128]{3,2,1,0:T(8,128)(2,1)}, bf16[2,2,256,128]{3,2,1,0:T(8,128)(2,1)S(1)}, u32[]{:S(2)}, u32[]{:S(2)}) collective-permute-start(bf16[2,2,256,128]{3,2,1,0:T(8,128)(2,1)} %get-tuple-element.42), channel_id=1, source_target_pairs={{0,2},{2,0},{4,6},{6,4},{8,10},{10,8},{12,14},{14,12},{16,18},{18,... | collective-permute-start | bytes 786440 | tf_op jit(solution)/shard_map/ppermute | solution.py:307
  70.5 1.9 %collective-permute-done.19.refs_0_ = bf16[256,512]{1,0:T(8,128)(2,1)S(1)} collective-permute-done((bf16[256,512]{1,0:T(8,128)(2,1)S(1)}, bf16[256,512]{1,0:T(8,128)(2,1)S(1)}, u32[]{:S(2)}, u32[]{:S(2)}) %collective-permute-start.19) | collective-permute-done | bytes 262176 | tf_op jit(solution)/shard_map/ppermute | solution.py:307
  72.4 2.2 %collective-permute-start.18 = (bf16[2,2,256,128]{3,2,1,0:T(8,128)(2,1)}, bf16[2,2,256,128]{3,2,1,0:T(8,128)(2,1)S(1)}, u32[]{:S(2)}, u32[]{:S(2)}) collective-permute-start(bf16[2,2,256,128]{3,2,1,0:T(8,128)(2,1)} %get-tuple-element.43), channel_id=1, source_target_pairs={{0,4},{2,6},{4,0},{6,2},{8,12},{10,14},{12,8},{14,10},{16,20},{18,... | collective-permute-start | bytes 786440 | tf_op jit(solution)/shard_map/ppermute | solution.py:307
  77.7 2.0 %collective-permute-start.22 = (bf16[1,2,256,128]{3,2,1,0:T(8,128)(2,1)}, bf16[1,2,256,128]{3,2,1,0:T(8,128)(2,1)}, u32[]{:S(2)}, u32[]{:S(2)}) collective-permute-start(bf16[1,2,256,128]{3,2,1,0:T(8,128)(2,1)} %get-tuple-element.47), channel_id=1, source_target_pairs={{0,4},{2,6},{4,0},{6,2},{8,12},{10,14},{12,8},{14,10},{16,20},{18,... | collective-permute-start | bytes 393224 | tf_op jit(solution)/shard_map/ppermute | solution.py:307
  79.9 3.0 %collective-permute-done.17.refs_5_ = bf16[2,2,256,128]{3,2,1,0:T(8,128)(2,1)S(1)} collective-permute-done((bf16[2,2,256,128]{3,2,1,0:T(8,128)(2,1)}, bf16[2,2,256,128]{3,2,1,0:T(8,128)(2,1)S(1)}, u32[]{:S(2)}, u32[]{:S(2)}) %collective-permute-start.17) | collective-permute-done | bytes 262176 | tf_op jit(solution)/shard_map/ppermute | solution.py:307
  82.8 2.0 %collective-permute-done.18.refs_6_ = bf16[2,2,256,128]{3,2,1,0:T(8,128)(2,1)S(1)} collective-permute-done((bf16[2,2,256,128]{3,2,1,0:T(8,128)(2,1)}, bf16[2,2,256,128]{3,2,1,0:T(8,128)(2,1)S(1)}, u32[]{:S(2)}, u32[]{:S(2)}) %collective-permute-start.18) | collective-permute-done | bytes 262176 | tf_op jit(solution)/shard_map/ppermute | solution.py:307
  85.2 2.1 %collective-permute-done.21.refs_9_ = bf16[1,2,256,128]{3,2,1,0:T(8,128)(2,1)S(1)} collective-permute-done((bf16[1,2,256,128]{3,2,1,0:T(8,128)(2,1)}, bf16[1,2,256,128]{3,2,1,0:T(8,128)(2,1)S(1)}, u32[]{:S(2)}, u32[]{:S(2)}) %collective-permute-start.21) | collective-permute-done | bytes 131104 | tf_op jit(solution)/shard_map/ppermute | solution.py:307
  87.3 2.4 %shard_map.99 = bf16[256,512]{1,0:T(8,128)(2,1)S(1)} custom-call(s32[181]{0:T(256)} %shard_map.92.lists_hbm, bf16[64,128,128]{2,1,0:T(8,128)(2,1)S(1)} %copy-done.1, bf16[1,2,256,128]{3,2,1,0:T(8,128)(2,1)} %copy-done.4, bf16[1,2,256,128]{3,2,1,0:T(8,128)(2,1)} %copy-done.5, bf16[1,2,256,128]{3,2,1,0:T(8,128)(2,1)} %copy-done.6, ...), custom_call_target="tpu_custom_call" | custom-call | flops 536870912 | bytes 4194304 | tf_op jit(solution)/shard_map/pallas_call | solution.py:287
  89.7 2.2 %all_gather.7.aggregated = bf16[512,512]{1,0:T(8,128)(2,1)S(1)} all-gather(bf16[256,512]{1,0:T(8,128)(2,1)S(1)} %shard_map.99), channel_id=1, replica_groups=mesh['node'=16,'col'=2] {'col'}, dimensions={0}, use_global_device_ids=true | all-gather | bytes 786432 | tf_op jit(solution)/shard_map/all_gather | solution.py:348
  (57 shorter events, 23.6 us)
Async XLA Ops:
  0.0 49.1 %copy-start = (bf16[256,512]{1,0:T(8,128)(2,1)S(1)}, bf16[256,512]{1,0:T(8,128)(2,1)}, u32[]{:S(2)}) copy-start(bf16[256,512]{1,0:T(8,128)(2,1)} %param.14) | copy-start | bytes 786436
  0.0 19.7 %collective-permute-start = (bf16[256,512]{1,0:T(8,128)(2,1)}, bf16[256,512]{1,0:T(8,128)(2,1)S(1)}, u32[]{:S(2)}, u32[]{:S(2)}) collective-permute-start(bf16[256,512]{1,0:T(8,128)(2,1)} %refs_1_.3), channel_id=1, source_target_pairs={{0,16},{2,18},{4,20},{6,22},{8,24},{10,26},{12,28},{14,30},{16,0},... | collective-permute-start | bytes 786440 | tf_op jit(solution)/shard_map/ppermute | solution.py:310
  4.0 15.7 %collective-permute-start.1 = (bf16[256,512]{1,0:T(8,128)(2,1)}, bf16[256,512]{1,0:T(8,128)(2,1)S(1)}, u32[]{:S(2)}, u32[]{:S(2)}) collective-permute-start(bf16[256,512]{1,0:T(8,128)(2,1)} %refs_1_.3), channel_id=1, source_target_pairs={{0,2},{2,0},{4,6},{6,4},{8,10},{10,8},{12,14},{14,12},{16,18},{18,... | collective-permute-start | bytes 786440 | tf_op jit(solution)/shard_map/ppermute | solution.py:307
  5.5 14.2 %collective-permute-start.2 = (bf16[256,512]{1,0:T(8,128)(2,1)}, bf16[256,512]{1,0:T(8,128)(2,1)S(1)}, u32[]{:S(2)}, u32[]{:S(2)}) collective-permute-start(bf16[256,512]{1,0:T(8,128)(2,1)} %refs_1_.3), channel_id=1, source_target_pairs={{0,4},{2,6},{4,0},{6,2},{8,12},{10,14},{12,8},{14,10},{16,20},{18,... | collective-permute-start | bytes 786440 | tf_op jit(solution)/shard_map/ppermute | solution.py:307
  7.1 12.7 %collective-permute-start.3 = (bf16[256,512]{1,0:T(8,128)(2,1)}, bf16[256,512]{1,0:T(8,128)(2,1)S(1)}, u32[]{:S(2)}, u32[]{:S(2)}) collective-permute-start(bf16[256,512]{1,0:T(8,128)(2,1)} %refs_1_.3), channel_id=1, source_target_pairs={{0,8},{2,10},{4,12},{6,14},{8,0},{10,2},{12,4},{14,6},{16,24},{18,... | collective-permute-start | bytes 786440 | tf_op jit(solution)/shard_map/ppermute | solution.py:307
  22.1 7.8 %collective-permute-start.5 = (bf16[1,2,256,128]{3,2,1,0:T(8,128)(2,1)}, bf16[1,2,256,128]{3,2,1,0:T(8,128)(2,1)S(1)}, u32[]{:S(2)}, u32[]{:S(2)}) collective-permute-start(bf16[1,2,256,128]{3,2,1,0:T(8,128)(2,1)} %get-tuple-element.30), channel_id=1, source_target_pairs={{0,12},{2,14},{4,8},{6,10},{8,4},{10,6},{12,0},{14,2},{16,28},{18,... | collective-permute-start | bytes 393224 | tf_op jit(solution)/shard_map/ppermute | solution.py:307
  22.8 21.5 %collective-permute-start.4 = (bf16[2,2,256,128]{3,2,1,0:T(8,128)(2,1)}, bf16[2,2,256,128]{3,2,1,0:T(8,128)(2,1)S(1)}, u32[]{:S(2)}, u32[]{:S(2)}) collective-permute-start(bf16[2,2,256,128]{3,2,1,0:T(8,128)(2,1)} %get-tuple-element.29), channel_id=1, source_target_pairs={{0,14},{2,12},{4,10},{6,8},{8,6},{10,4},{12,2},{14,0},{16,30},{18,... | collective-permute-start | bytes 786440 | tf_op jit(solution)/shard_map/ppermute | solution.py:307
  25.4 12.8 %collective-permute-start.6 = (bf16[1,2,256,128]{3,2,1,0:T(8,128)(2,1)}, bf16[1,2,256,128]{3,2,1,0:T(8,128)(2,1)S(1)}, u32[]{:S(2)}, u32[]{:S(2)}) collective-permute-start(bf16[1,2,256,128]{3,2,1,0:T(8,128)(2,1)} %get-tuple-element.31), channel_id=1, source_target_pairs={{0,10},{2,8},{4,14},{6,12},{8,2},{10,0},{12,6},{14,4},{16,26},{18,... | collective-permute-start | bytes 393224 | tf_op jit(solution)/shard_map/ppermute | solution.py:307
  26.6 17.7 %collective-permute-start.7 = (bf16[2,2,256,128]{3,2,1,0:T(8,128)(2,1)}, bf16[2,2,256,128]{3,2,1,0:T(8,128)(2,1)S(1)}, u32[]{:S(2)}, u32[]{:S(2)}) collective-permute-start(bf16[2,2,256,128]{3,2,1,0:T(8,128)(2,1)} %get-tuple-element.32), channel_id=1, source_target_pairs={{0,8},{2,10},{4,12},{6,14},{8,0},{10,2},{12,4},{14,6},{16,24},{18,... | collective-permute-start | bytes 786440 | tf_op jit(solution)/shard_map/ppermute | solution.py:307
  28.0 16.2 %collective-permute-start.9 = (bf16[2,2,256,128]{3,2,1,0:T(8,128)(2,1)}, bf16[2,2,256,128]{3,2,1,0:T(8,128)(2,1)S(1)}, u32[]{:S(2)}, u32[]{:S(2)}) collective-permute-start(bf16[2,2,256,128]{3,2,1,0:T(8,128)(2,1)} %get-tuple-element.34), channel_id=1, source_target_pairs={{0,2},{2,0},{4,6},{6,4},{8,10},{10,8},{12,14},{14,12},{16,18},{18,... | collective-permute-start | bytes 786440 | tf_op jit(solution)/shard_map/ppermute | solution.py:307
  30.0 14.3 %collective-permute-start.10 = (bf16[2,2,256,128]{3,2,1,0:T(8,128)(2,1)}, bf16[2,2,256,128]{3,2,1,0:T(8,128)(2,1)S(1)}, u32[]{:S(2)}, u32[]{:S(2)}) collective-permute-start(bf16[2,2,256,128]{3,2,1,0:T(8,128)(2,1)} %get-tuple-element.35), channel_id=1, source_target_pairs={{0,4},{2,6},{4,0},{6,2},{8,12},{10,14},{12,8},{14,10},{16,20},{18,... | collective-permute-start | bytes 786440 | tf_op jit(solution)/shard_map/ppermute | solution.py:307
  38.2 6.1 %collective-permute-start.8 = (bf16[1,2,256,128]{3,2,1,0:T(8,128)(2,1)}, bf16[1,2,256,128]{3,2,1,0:T(8,128)(2,1)S(1)}, u32[]{:S(2)}, u32[]{:S(2)}) collective-permute-start(bf16[1,2,256,128]{3,2,1,0:T(8,128)(2,1)} %get-tuple-element.33), channel_id=1, source_target_pairs={{0,6},{2,4},{4,2},{6,0},{8,14},{10,12},{12,10},{14,8},{16,22},{18,... | collective-permute-start | bytes 393224 | tf_op jit(solution)/shard_map/ppermute | solution.py:307
  49.5 15.0 %collective-permute-start.15 = (bf16[256,512]{1,0:T(8,128)(2,1)S(1)}, bf16[256,512]{1,0:T(8,128)(2,1)S(1)}, u32[]{:S(2)}, u32[]{:S(2)}) collective-permute-start(bf16[256,512]{1,0:T(8,128)(2,1)S(1)} %fusion.2.refs_0_), channel_id=1, source_target_pairs={{0,16},{2,18},{4,20},{6,22},{8,24},{10,26},{12,28},{14,30},{16,0},... | collective-permute-start | bytes 786440 | tf_op jit(solution)/shard_map/ppermute | solution.py:310
  51.6 13.3 %collective-permute-start.14 = (bf16[256,512]{1,0:T(8,128)(2,1)S(1)}, bf16[256,512]{1,0:T(8,128)(2,1)S(1)}, u32[]{:S(2)}, u32[]{:S(2)}) collective-permute-start(bf16[256,512]{1,0:T(8,128)(2,1)S(1)} %fusion.2.refs_0_), channel_id=1, source_target_pairs={{0,8},{2,10},{4,12},{6,14},{8,0},{10,2},{12,4},{14,6},{16,24},{18,... | collective-permute-start | bytes 786440 | tf_op jit(solution)/shard_map/ppermute | solution.py:307
  54.5 13.3 %collective-permute-start.11 = (bf16[1,2,256,128]{3,2,1,0:T(8,128)(2,1)}, bf16[1,2,256,128]{3,2,1,0:T(8,128)(2,1)S(1)}, u32[]{:S(2)}, u32[]{:S(2)}) collective-permute-start(bf16[1,2,256,128]{3,2,1,0:T(8,128)(2,1)} %get-tuple-element.37), channel_id=1, source_target_pairs={{0,6},{2,4},{4,2},{6,0},{8,14},{10,12},{12,10},{14,8},{16,22},{18,... | collective-permute-start | bytes 393224 | tf_op jit(solution)/shard_map/ppermute | solution.py:307
  57.3 18.8 %collective-permute-start.12 = (bf16[1,2,256,128]{3,2,1,0:T(8,128)(2,1)}, bf16[1,2,256,128]{3,2,1,0:T(8,128)(2,1)S(1)}, u32[]{:S(2)}, u32[]{:S(2)}) collective-permute-start(bf16[1,2,256,128]{3,2,1,0:T(8,128)(2,1)} %get-tuple-element.38), channel_id=1, source_target_pairs={{0,2},{2,0},{4,6},{6,4},{8,10},{10,8},{12,14},{14,12},{16,18},{18,... | collective-permute-start | bytes 393224 | tf_op jit(solution)/shard_map/ppermute | solution.py:307
  57.7 18.9 %collective-permute-start.13 = (bf16[1,2,256,128]{3,2,1,0:T(8,128)(2,1)}, bf16[1,2,256,128]{3,2,1,0:T(8,128)(2,1)S(1)}, u32[]{:S(2)}, u32[]{:S(2)}) collective-permute-start(bf16[1,2,256,128]{3,2,1,0:T(8,128)(2,1)} %get-tuple-element.39), channel_id=1, source_target_pairs={{0,4},{2,6},{4,0},{6,2},{8,12},{10,14},{12,8},{14,10},{16,20},{18,... | collective-permute-start | bytes 393224 | tf_op jit(solution)/shard_map/ppermute | solution.py:307
  64.5 7.9 %collective-permute-start.19 = (bf16[256,512]{1,0:T(8,128)(2,1)S(1)}, bf16[256,512]{1,0:T(8,128)(2,1)S(1)}, u32[]{:S(2)}, u32[]{:S(2)}) collective-permute-start(bf16[256,512]{1,0:T(8,128)(2,1)S(1)} %collective-permute-done.15.refs_1_), channel_id=1, source_target_pairs={{0,8},{2,10},{4,12},{6,14},{8,0},{10,2},{12,4},{14,6},{16,24},{18,... | collective-permute-start | bytes 786440 | tf_op jit(solution)/shard_map/ppermute | solution.py:307
  66.6 11.1 %collective-permute-start.16 = (bf16[2,2,256,128]{3,2,1,0:T(8,128)(2,1)}, bf16[2,2,256,128]{3,2,1,0:T(8,128)(2,1)S(1)}, u32[]{:S(2)}, u32[]{:S(2)}) collective-permute-start(bf16[2,2,256,128]{3,2,1,0:T(8,128)(2,1)} %get-tuple-element.41), channel_id=1, source_target_pairs={{0,6},{2,4},{4,2},{6,0},{8,14},{10,12},{12,10},{14,8},{16,22},{18,... | collective-permute-start | bytes 786440 | tf_op jit(solution)/shard_map/ppermute | solution.py:307
  68.5 14.4 %collective-permute-start.17 = (bf16[2,2,256,128]{3,2,1,0:T(8,128)(2,1)}, bf16[2,2,256,128]{3,2,1,0:T(8,128)(2,1)S(1)}, u32[]{:S(2)}, u32[]{:S(2)}) collective-permute-start(bf16[2,2,256,128]{3,2,1,0:T(8,128)(2,1)} %get-tuple-element.42), channel_id=1, source_target_pairs={{0,2},{2,0},{4,6},{6,4},{8,10},{10,8},{12,14},{14,12},{16,18},{18,... | collective-permute-start | bytes 786440 | tf_op jit(solution)/shard_map/ppermute | solution.py:307
  72.4 12.4 %collective-permute-start.18 = (bf16[2,2,256,128]{3,2,1,0:T(8,128)(2,1)}, bf16[2,2,256,128]{3,2,1,0:T(8,128)(2,1)S(1)}, u32[]{:S(2)}, u32[]{:S(2)}) collective-permute-start(bf16[2,2,256,128]{3,2,1,0:T(8,128)(2,1)} %get-tuple-element.43), channel_id=1, source_target_pairs={{0,4},{2,6},{4,0},{6,2},{8,12},{10,14},{12,8},{14,10},{16,20},{18,... | collective-permute-start | bytes 786440 | tf_op jit(solution)/shard_map/ppermute | solution.py:307
  76.2 9.1 %collective-permute-start.20 = (bf16[1,2,256,128]{3,2,1,0:T(8,128)(2,1)}, bf16[1,2,256,128]{3,2,1,0:T(8,128)(2,1)S(1)}, u32[]{:S(2)}, u32[]{:S(2)}) collective-permute-start(bf16[1,2,256,128]{3,2,1,0:T(8,128)(2,1)} %get-tuple-element.45), channel_id=1, source_target_pairs={{0,6},{2,4},{4,2},{6,0},{8,14},{10,12},{12,10},{14,8},{16,22},{18,... | collective-permute-start | bytes 393224 | tf_op jit(solution)/shard_map/ppermute | solution.py:307
  76.6 10.7 %collective-permute-start.21 = (bf16[1,2,256,128]{3,2,1,0:T(8,128)(2,1)}, bf16[1,2,256,128]{3,2,1,0:T(8,128)(2,1)S(1)}, u32[]{:S(2)}, u32[]{:S(2)}) collective-permute-start(bf16[1,2,256,128]{3,2,1,0:T(8,128)(2,1)} %get-tuple-element.46), channel_id=1, source_target_pairs={{0,2},{2,0},{4,6},{6,4},{8,10},{10,8},{12,14},{14,12},{16,18},{18,... | collective-permute-start | bytes 393224 | tf_op jit(solution)/shard_map/ppermute | solution.py:307
  77.7 9.6 %collective-permute-start.22 = (bf16[1,2,256,128]{3,2,1,0:T(8,128)(2,1)}, bf16[1,2,256,128]{3,2,1,0:T(8,128)(2,1)}, u32[]{:S(2)}, u32[]{:S(2)}) collective-permute-start(bf16[1,2,256,128]{3,2,1,0:T(8,128)(2,1)} %get-tuple-element.47), channel_id=1, source_target_pairs={{0,4},{2,6},{4,0},{6,2},{8,12},{10,14},{12,8},{14,10},{16,20},{18,... | collective-permute-start | bytes 393224 | tf_op jit(solution)/shard_map/ppermute | solution.py:307
  (8 other events, 49.3 us)

commit v3 on v1

--- a/solution.py
+++ b/solution.py
@@ -13,9 +13,9 @@
 NEAR = (0, 1, 2, 4)
 PASSED = {7: 0, 4: 1, 1: 2, 2: 4}
 STEPS = (7, 6, 3, 4, 5, 1, 2)
-DEPTH = 4
+DEPTH = 8
 RELAY_WORK = 50_000_000_000
-WIDTH = 4
+WIDTH = 2
 SMEM = pl.BlockSpec(memory_space=pltpu.SMEM)
 VMEM = pl.BlockSpec(memory_space=pltpu.VMEM)
 HBM = pl.BlockSpec(memory_space=pltpu.HBM)

time: 93.9 us -> 92.9 us (0.989)
  starting transfers between devices: 30.2 us -> 33.6 us
  waiting for transfers between devices: 27.4 us -> 25.2 us
  Pallas kernels: 18.9 us -> 17.5 us
    ppermute x21, starting transfers between devices: 24.3 us -> 27.7 us  [to_member(): return lax.ppermute(array, 'node', [(n, n ^ step) for n in range(nodes)])]
    ppermute x21, waiting for transfers between devices: 21.1 us -> 19.5 us  [to_member(): return lax.ppermute(array, 'node', [(n, n ^ step) for n in range(nodes)])]
where the time goes in v3:
time: 92.9 us; the launch traced here: 92.3 us
  starting transfers between devices  33.6 us (36%)
  waiting for transfers between devices  25.2 us (27%)
  Pallas kernels  17.5 us (19%)
  blocking collectives  13.1 us (14%)
  local copies, waits for them, and re-layouts  1.92 us (2%)
    ppermute x21, starting transfers between devices, to_member(): return lax.ppermute(array, 'node', [(n, n ^ step) for n in range(nodes)])  27.7 us
    ppermute x21, waiting for transfers between devices, to_member(): return lax.ppermute(array, 'node', [(n, n ^ step) for n in range(nodes)])  19.5 us
    all_to_all x1, blocking collectives, exchange(): lax.all_to_all(array, 'node', split_axis=0, concat_axis=0, tiled=True, ax...  8.75 us
    pallas_call x4, Pallas kernels, pack(): pl.pallas_call(functools.partial(pack_kernel, cubes, tuple(held), message...  7.01 us
    ppermute x2, starting transfers between devices, gather_sums(): lax.ppermute(feat_t, 'node', [(n, (n - unit * GROUP) % nodes) for n in ra...  5.86 us
    ppermute x2, waiting for transfers between devices, gather_sums(): lax.ppermute(feat_t, 'node', [(n, (n - unit * GROUP) % nodes) for n in ra...  5.7 us
    pallas_call x2, Pallas kernels, aggregate(): pl.pallas_call(functools.partial(aggregate_kernel, cubes, limit, messages...  5.06 us
    all_gather x2, blocking collectives, gather_sums(): return lax.all_gather(local, 'col', axis=0, tiled=True)  4.36 us
  transfers between devices with their start and end apart: 23, of which 11 were waited for; matrix products, arithmetic and copies ran while one was open for 0% of the time, Pallas kernels for 10%

profile of v3, /device:TPU:0, one launch (start us, length us, event | category | flops | bytes accessed | tf_op | source)
XLA Modules:
  0.0 92.3 jit_solution(10416700110514433978)
XLA Ops:
  0.0 4.0 %collective-permute-start = (bf16[256,512]{1,0:T(8,128)(2,1)}, bf16[256,512]{1,0:T(8,128)(2,1)S(1)}, u32[]{:S(2)}, u32[]{:S(2)}) collective-permute-start(bf16[256,512]{1,0:T(8,128)(2,1)} %refs_1_.3), channel_id=1, source_target_pairs={{0,16},{2,18},{4,20},{6,22},{8,24},{10,26},{12,28},{14,30},{16,0},... | collective-permute-start | bytes 786440 | tf_op jit(solution)/shard_map/ppermute | solution.py:310
  5.5 1.5 %collective-permute-start.2 = (bf16[256,512]{1,0:T(8,128)(2,1)}, bf16[256,512]{1,0:T(8,128)(2,1)S(1)}, u32[]{:S(2)}, u32[]{:S(2)}) collective-permute-start(bf16[256,512]{1,0:T(8,128)(2,1)} %refs_1_.3), channel_id=1, source_target_pairs={{0,4},{2,6},{4,0},{6,2},{8,12},{10,14},{12,8},{14,10},{16,20},{18,... | collective-permute-start | bytes 786440 | tf_op jit(solution)/shard_map/ppermute | solution.py:307
  7.1 1.6 %collective-permute-start.3 = (bf16[256,512]{1,0:T(8,128)(2,1)}, bf16[256,512]{1,0:T(8,128)(2,1)S(1)}, u32[]{:S(2)}, u32[]{:S(2)}) collective-permute-start(bf16[256,512]{1,0:T(8,128)(2,1)} %refs_1_.3), channel_id=1, source_target_pairs={{0,8},{2,10},{4,12},{6,14},{8,0},{10,2},{12,4},{14,6},{16,24},{18,... | collective-permute-start | bytes 786440 | tf_op jit(solution)/shard_map/ppermute | solution.py:307
  9.3 1.5 %shard_map.91.words_ref = s32[8,2]{1,0:T(8,128)} custom-call(s32[1]{0:T(128)S(6)} %copy.38.count_ref, s32[64]{0:T(128)} %cols_ref.3), custom_call_target="tpu_custom_call" | custom-call | tf_op jit(solution)/shard_map/pallas_call | solution.py:121
  10.8 8.7 %all_to_all.11 = s32[8,1,2]{2,1,0:T(1,128)S(1)} all-to-all(s32[8,1,2]{2,1,0:T(1,128)} %bitcast.9), channel_id=1, replica_groups={{0,2,4,6,8,10,12,14},{16,18,20,22,24,26,28,30},{1,3,5,7,9,11,13,15},{17..., dimensions={0} | all-to-all | bytes 128 | tf_op jit(solution)/shard_map/all_to_all | solution.py:140
  19.8 2.4 %shard_map.93 = (bf16[2,2,256,128]{3,2,1,0:T(8,128)(2,1)}, bf16[1,2,256,128]{3,2,1,0:T(8,128)(2,1)}, bf16[1,2,256,128]{3,2,1,0:T(8,128)(2,1)}, bf16[2,2,256,128]...) custom-call(s32[8,2]{1,0:T(8,128)S(1)} %copy.31.words_ref, ...), custom_call_target="tpu_custom_call" | custom-call | tf_op jit(solution)/shard_map/pallas_call | solution.py:188
  22.8 2.6 %collective-permute-start.4 = (bf16[2,2,256,128]{3,2,1,0:T(8,128)(2,1)}, bf16[2,2,256,128]{3,2,1,0:T(8,128)(2,1)S(1)}, u32[]{:S(2)}, u32[]{:S(2)}) collective-permute-start(bf16[2,2,256,128]{3,2,1,0:T(8,128)(2,1)} %get-tuple-element.29), channel_id=1, source_target_pairs={{0,14},{2,12},{4,10},{6,8},{8,6},{10,4},{12,2},{14,0},{16,30},{18,... | collective-permute-start | bytes 786440 | tf_op jit(solution)/shard_map/ppermute | solution.py:307
  28.3 2.3 %collective-permute-done.5.refs_1_ = bf16[1,2,256,128]{3,2,1,0:T(8,128)(2,1)S(1)} collective-permute-done((bf16[1,2,256,128]{3,2,1,0:T(8,128)(2,1)}, bf16[1,2,256,128]{3,2,1,0:T(8,128)(2,1)S(1)}, u32[]{:S(2)}, u32[]{:S(2)}) %collective-permute-start.5) | collective-permute-done | bytes 131104 | tf_op jit(solution)/shard_map/ppermute | solution.py:307
  31.4 2.0 %shard_map.92.lists_hbm = s32[205]{0:T(256)} custom-call(s32[1]{0:T(128)S(6)} %copy.38.count_ref, s32[64]{0:T(128)} %rows_ref.1, s32[64]{0:T(128)} %cols_ref.3, s32[8,2]{1,0:T(8,128)} %shard_map.91.words_ref), custom_call_target="tpu_custom_call" | custom-call | tf_op jit(solution)/shard_map/pallas_call | solution.py:127
  37.8 4.8 %collective-permute-done.8.refs_4_ = bf16[1,2,256,128]{3,2,1,0:T(8,128)(2,1)S(1)} collective-permute-done((bf16[1,2,256,128]{3,2,1,0:T(8,128)(2,1)}, bf16[1,2,256,128]{3,2,1,0:T(8,128)(2,1)S(1)}, u32[]{:S(2)}, u32[]{:S(2)}) %collective-permute-start.8) | collective-permute-done | bytes 131104 | tf_op jit(solution)/shard_map/ppermute | solution.py:307
  43.8 2.7 %shard_map.95 = bf16[256,512]{1,0:T(8,128)(2,1)S(1)} custom-call(s32[205]{0:T(256)} %shard_map.92.lists_hbm, bf16[64,128,128]{2,1,0:T(8,128)(2,1)} %tiles.3, bf16[2,2,256,128]{3,2,1,0:T(8,128)(2,1)S(1)} %collective-permute-done.4.refs_0_, bf16[1,2,256,128]{3,2,1,0:T(8,128)(2,1)S(1)} %collective-permute-done.5.refs_1_, ...), custom_call_target="tpu_custom_call" | custom-call | flops 536870912 | bytes 4194304 | tf_op jit(solution)/shard_map/pallas_call | solution.py:287
  46.4 2.2 %all_gather.6 = bf16[512,512]{1,0:T(8,128)(2,1)S(1)} all-gather(bf16[256,512]{1,0:T(8,128)(2,1)S(1)} %shard_map.95), channel_id=1, replica_groups=mesh['node'=16,'col'=2] {'col'}, dimensions={0}, use_global_device_ids=true | all-gather | bytes 786432 | tf_op jit(solution)/shard_map/all_gather | solution.py:348
  48.9 1.8 %collective-permute-start.15 = (bf16[256,512]{1,0:T(8,128)(2,1)S(1)}, bf16[256,512]{1,0:T(8,128)(2,1)S(1)}, u32[]{:S(2)}, u32[]{:S(2)}) collective-permute-start(bf16[256,512]{1,0:T(8,128)(2,1)S(1)} %fusion.2.refs_0_), channel_id=1, source_target_pairs={{0,16},{2,18},{4,20},{6,22},{8,24},{10,26},{12,28},{14,30},{16,0},... | collective-permute-start | bytes 786440 | tf_op jit(solution)/shard_map/ppermute | solution.py:310
  50.7 1.9 %collective-permute-start.14 = (bf16[256,512]{1,0:T(8,128)(2,1)S(1)}, bf16[256,512]{1,0:T(8,128)(2,1)S(1)}, u32[]{:S(2)}, u32[]{:S(2)}) collective-permute-start(bf16[256,512]{1,0:T(8,128)(2,1)S(1)} %fusion.2.refs_0_), channel_id=1, source_target_pairs={{0,8},{2,10},{4,12},{6,14},{8,0},{10,2},{12,4},{14,6},{16,24},{18,... | collective-permute-start | bytes 786440 | tf_op jit(solution)/shard_map/ppermute | solution.py:307
  54.1 2.7 %collective-permute-start.11 = (bf16[1,2,256,128]{3,2,1,0:T(8,128)(2,1)}, bf16[1,2,256,128]{3,2,1,0:T(8,128)(2,1)S(1)}, u32[]{:S(2)}, u32[]{:S(2)}) collective-permute-start(bf16[1,2,256,128]{3,2,1,0:T(8,128)(2,1)} %get-tuple-element.37), channel_id=1, source_target_pairs={{0,6},{2,4},{4,2},{6,0},{8,14},{10,12},{12,10},{14,8},{16,22},{18,... | collective-permute-start | bytes 393224 | tf_op jit(solution)/shard_map/ppermute | solution.py:307
  58.3 5.7 %collective-permute-done.15.refs_1_ = bf16[256,512]{1,0:T(8,128)(2,1)S(1)} collective-permute-done((bf16[256,512]{1,0:T(8,128)(2,1)S(1)}, bf16[256,512]{1,0:T(8,128)(2,1)S(1)}, u32[]{:S(2)}, u32[]{:S(2)}) %collective-permute-start.15) | collective-permute-done | bytes 262176 | tf_op jit(solution)/shard_map/ppermute | solution.py:310
  64.0 1.7 %shard_map.97 = (bf16[2,2,256,128]{3,2,1,0:T(8,128)(2,1)}, bf16[2,2,256,128]{3,2,1,0:T(8,128)(2,1)}, bf16[2,2,256,128]{3,2,1,0:T(8,128)(2,1)}, bf16[2,2,256,128]{3,2,1,0:T(8,128)(2,1)}) custom-call(s32[8,2]{1,0:T(8,128)S(1)} %copy.31.words_ref, bf16[256,512]{1,0:T(8,128)(2,1)S(1)} %collective-permute-done.14.refs_0_, ...), custom_call_target="tpu_custom_call" | custom-call | flops 49999998976 | tf_op jit(solution)/shard_map/pallas_call | solution.py:188
  65.7 3.1 %collective-permute-start.16 = (bf16[2,2,256,128]{3,2,1,0:T(8,128)(2,1)}, bf16[2,2,256,128]{3,2,1,0:T(8,128)(2,1)S(1)}, u32[]{:S(2)}, u32[]{:S(2)}) collective-permute-start(bf16[2,2,256,128]{3,2,1,0:T(8,128)(2,1)} %get-tuple-element.41), channel_id=1, source_target_pairs={{0,6},{2,4},{4,2},{6,0},{8,14},{10,12},{12,10},{14,8},{16,22},{18,... | collective-permute-start | bytes 786440 | tf_op jit(solution)/shard_map/ppermute | solution.py:307
  69.4 2.2 %collective-permute-done.19.refs_0_ = bf16[256,512]{1,0:T(8,128)(2,1)S(1)} collective-permute-done((bf16[256,512]{1,0:T(8,128)(2,1)S(1)}, bf16[256,512]{1,0:T(8,128)(2,1)S(1)}, u32[]{:S(2)}, u32[]{:S(2)}) %collective-permute-start.19) | collective-permute-done | bytes 262176 | tf_op jit(solution)/shard_map/ppermute | solution.py:307
  73.9 2.7 %collective-permute-start.20 = (bf16[1,2,256,128]{3,2,1,0:T(8,128)(2,1)}, bf16[1,2,256,128]{3,2,1,0:T(8,128)(2,1)S(1)}, u32[]{:S(2)}, u32[]{:S(2)}) collective-permute-start(bf16[1,2,256,128]{3,2,1,0:T(8,128)(2,1)} %get-tuple-element.45), channel_id=1, source_target_pairs={{0,6},{2,4},{4,2},{6,0},{8,14},{10,12},{12,10},{14,8},{16,22},{18,... | collective-permute-start | bytes 393224 | tf_op jit(solution)/shard_map/ppermute | solution.py:307
  78.9 2.5 %collective-permute-done.17.refs_5_ = bf16[2,2,256,128]{3,2,1,0:T(8,128)(2,1)S(1)} collective-permute-done((bf16[2,2,256,128]{3,2,1,0:T(8,128)(2,1)}, bf16[2,2,256,128]{3,2,1,0:T(8,128)(2,1)S(1)}, u32[]{:S(2)}, u32[]{:S(2)}) %collective-permute-start.17) | collective-permute-done | bytes 262176 | tf_op jit(solution)/shard_map/ppermute | solution.py:307
  81.4 2.5 %collective-permute-done.18.refs_6_ = bf16[2,2,256,128]{3,2,1,0:T(8,128)(2,1)S(1)} collective-permute-done((bf16[2,2,256,128]{3,2,1,0:T(8,128)(2,1)}, bf16[2,2,256,128]{3,2,1,0:T(8,128)(2,1)S(1)}, u32[]{:S(2)}, u32[]{:S(2)}) %collective-permute-start.18) | collective-permute-done | bytes 262176 | tf_op jit(solution)/shard_map/ppermute | solution.py:307
  86.6 2.4 %shard_map.99 = bf16[256,512]{1,0:T(8,128)(2,1)S(1)} custom-call(s32[205]{0:T(256)} %shard_map.92.lists_hbm, bf16[64,128,128]{2,1,0:T(8,128)(2,1)S(1)} %copy-done.1, bf16[1,2,256,128]{3,2,1,0:T(8,128)(2,1)} %copy-done.4, bf16[1,2,256,128]{3,2,1,0:T(8,128)(2,1)} %copy-done.5, bf16[1,2,256,128]{3,2,1,0:T(8,128)(2,1)} %copy-done.6, ...), custom_call_target="tpu_custom_call" | custom-call | flops 536870912 | bytes 4194304 | tf_op jit(solution)/shard_map/pallas_call | solution.py:287
  89.0 2.2 %all_gather.7.aggregated = bf16[512,512]{1,0:T(8,128)(2,1)S(1)} all-gather(bf16[256,512]{1,0:T(8,128)(2,1)S(1)} %shard_map.99), channel_id=1, replica_groups=mesh['node'=16,'col'=2] {'col'}, dimensions={0}, use_global_device_ids=true | all-gather | bytes 786432 | tf_op jit(solution)/shard_map/all_gather | solution.py:348
  (57 shorter events, 23.8 us)
Async XLA Ops:
  0.0 48.6 %copy-start = (bf16[256,512]{1,0:T(8,128)(2,1)S(1)}, bf16[256,512]{1,0:T(8,128)(2,1)}, u32[]{:S(2)}) copy-start(bf16[256,512]{1,0:T(8,128)(2,1)} %param.14) | copy-start | bytes 786436
  0.0 19.7 %collective-permute-start = (bf16[256,512]{1,0:T(8,128)(2,1)}, bf16[256,512]{1,0:T(8,128)(2,1)S(1)}, u32[]{:S(2)}, u32[]{:S(2)}) collective-permute-start(bf16[256,512]{1,0:T(8,128)(2,1)} %refs_1_.3), channel_id=1, source_target_pairs={{0,16},{2,18},{4,20},{6,22},{8,24},{10,26},{12,28},{14,30},{16,0},... | collective-permute-start | bytes 786440 | tf_op jit(solution)/shard_map/ppermute | solution.py:310
  4.0 15.7 %collective-permute-start.1 = (bf16[256,512]{1,0:T(8,128)(2,1)}, bf16[256,512]{1,0:T(8,128)(2,1)S(1)}, u32[]{:S(2)}, u32[]{:S(2)}) collective-permute-start(bf16[256,512]{1,0:T(8,128)(2,1)} %refs_1_.3), channel_id=1, source_target_pairs={{0,2},{2,0},{4,6},{6,4},{8,10},{10,8},{12,14},{14,12},{16,18},{18,... | collective-permute-start | bytes 786440 | tf_op jit(solution)/shard_map/ppermute | solution.py:307
  5.5 14.2 %collective-permute-start.2 = (bf16[256,512]{1,0:T(8,128)(2,1)}, bf16[256,512]{1,0:T(8,128)(2,1)S(1)}, u32[]{:S(2)}, u32[]{:S(2)}) collective-permute-start(bf16[256,512]{1,0:T(8,128)(2,1)} %refs_1_.3), channel_id=1, source_target_pairs={{0,4},{2,6},{4,0},{6,2},{8,12},{10,14},{12,8},{14,10},{16,20},{18,... | collective-permute-start | bytes 786440 | tf_op jit(solution)/shard_map/ppermute | solution.py:307
  7.1 12.7 %collective-permute-start.3 = (bf16[256,512]{1,0:T(8,128)(2,1)}, bf16[256,512]{1,0:T(8,128)(2,1)S(1)}, u32[]{:S(2)}, u32[]{:S(2)}) collective-permute-start(bf16[256,512]{1,0:T(8,128)(2,1)} %refs_1_.3), channel_id=1, source_target_pairs={{0,8},{2,10},{4,12},{6,14},{8,0},{10,2},{12,4},{14,6},{16,24},{18,... | collective-permute-start | bytes 786440 | tf_op jit(solution)/shard_map/ppermute | solution.py:307
  22.1 8.5 %collective-permute-start.5 = (bf16[1,2,256,128]{3,2,1,0:T(8,128)(2,1)}, bf16[1,2,256,128]{3,2,1,0:T(8,128)(2,1)S(1)}, u32[]{:S(2)}, u32[]{:S(2)}) collective-permute-start(bf16[1,2,256,128]{3,2,1,0:T(8,128)(2,1)} %get-tuple-element.30), channel_id=1, source_target_pairs={{0,12},{2,14},{4,8},{6,10},{8,4},{10,6},{12,0},{14,2},{16,28},{18,... | collective-permute-start | bytes 393224 | tf_op jit(solution)/shard_map/ppermute | solution.py:307
  22.8 19.8 %collective-permute-start.4 = (bf16[2,2,256,128]{3,2,1,0:T(8,128)(2,1)}, bf16[2,2,256,128]{3,2,1,0:T(8,128)(2,1)S(1)}, u32[]{:S(2)}, u32[]{:S(2)}) collective-permute-start(bf16[2,2,256,128]{3,2,1,0:T(8,128)(2,1)} %get-tuple-element.29), channel_id=1, source_target_pairs={{0,14},{2,12},{4,10},{6,8},{8,6},{10,4},{12,2},{14,0},{16,30},{18,... | collective-permute-start | bytes 786440 | tf_op jit(solution)/shard_map/ppermute | solution.py:307
  25.4 11.0 %collective-permute-start.6 = (bf16[1,2,256,128]{3,2,1,0:T(8,128)(2,1)}, bf16[1,2,256,128]{3,2,1,0:T(8,128)(2,1)S(1)}, u32[]{:S(2)}, u32[]{:S(2)}) collective-permute-start(bf16[1,2,256,128]{3,2,1,0:T(8,128)(2,1)} %get-tuple-element.31), channel_id=1, source_target_pairs={{0,6},{2,4},{4,2},{6,0},{8,14},{10,12},{12,10},{14,8},{16,22},{18,... | collective-permute-start | bytes 393224 | tf_op jit(solution)/shard_map/ppermute | solution.py:307
  26.9 15.7 %collective-permute-start.7 = (bf16[2,2,256,128]{3,2,1,0:T(8,128)(2,1)}, bf16[2,2,256,128]{3,2,1,0:T(8,128)(2,1)S(1)}, u32[]{:S(2)}, u32[]{:S(2)}) collective-permute-start(bf16[2,2,256,128]{3,2,1,0:T(8,128)(2,1)} %get-tuple-element.32), channel_id=1, source_target_pairs={{0,8},{2,10},{4,12},{6,14},{8,0},{10,2},{12,4},{14,6},{16,24},{18,... | collective-permute-start | bytes 786440 | tf_op jit(solution)/shard_map/ppermute | solution.py:307
  27.1 16.6 %collective-permute-start.9 = (bf16[2,2,256,128]{3,2,1,0:T(8,128)(2,1)}, bf16[2,2,256,128]{3,2,1,0:T(8,128)(2,1)S(1)}, u32[]{:S(2)}, u32[]{:S(2)}) collective-permute-start(bf16[2,2,256,128]{3,2,1,0:T(8,128)(2,1)} %get-tuple-element.34), channel_id=1, source_target_pairs={{0,2},{2,0},{4,6},{6,4},{8,10},{10,8},{12,14},{14,12},{16,18},{18,... | collective-permute-start | bytes 786440 | tf_op jit(solution)/shard_map/ppermute | solution.py:307
  30.6 13.1 %collective-permute-start.10 = (bf16[2,2,256,128]{3,2,1,0:T(8,128)(2,1)}, bf16[2,2,256,128]{3,2,1,0:T(8,128)(2,1)S(1)}, u32[]{:S(2)}, u32[]{:S(2)}) collective-permute-start(bf16[2,2,256,128]{3,2,1,0:T(8,128)(2,1)} %get-tuple-element.35), channel_id=1, source_target_pairs={{0,4},{2,6},{4,0},{6,2},{8,12},{10,14},{12,8},{14,10},{16,20},{18,... | collective-permute-start | bytes 786440 | tf_op jit(solution)/shard_map/ppermute | solution.py:307
  36.4 6.2 %collective-permute-start.8 = (bf16[1,2,256,128]{3,2,1,0:T(8,128)(2,1)}, bf16[1,2,256,128]{3,2,1,0:T(8,128)(2,1)S(1)}, u32[]{:S(2)}, u32[]{:S(2)}) collective-permute-start(bf16[1,2,256,128]{3,2,1,0:T(8,128)(2,1)} %get-tuple-element.33), channel_id=1, source_target_pairs={{0,10},{2,8},{4,14},{6,12},{8,2},{10,0},{12,6},{14,4},{16,26},{18,... | collective-permute-start | bytes 393224 | tf_op jit(solution)/shard_map/ppermute | solution.py:307
  48.9 15.0 %collective-permute-start.15 = (bf16[256,512]{1,0:T(8,128)(2,1)S(1)}, bf16[256,512]{1,0:T(8,128)(2,1)S(1)}, u32[]{:S(2)}, u32[]{:S(2)}) collective-permute-start(bf16[256,512]{1,0:T(8,128)(2,1)S(1)} %fusion.2.refs_0_), channel_id=1, source_target_pairs={{0,16},{2,18},{4,20},{6,22},{8,24},{10,26},{12,28},{14,30},{16,0},... | collective-permute-start | bytes 786440 | tf_op jit(solution)/shard_map/ppermute | solution.py:310
  50.7 13.2 %collective-permute-start.14 = (bf16[256,512]{1,0:T(8,128)(2,1)S(1)}, bf16[256,512]{1,0:T(8,128)(2,1)S(1)}, u32[]{:S(2)}, u32[]{:S(2)}) collective-permute-start(bf16[256,512]{1,0:T(8,128)(2,1)S(1)} %fusion.2.refs_0_), channel_id=1, source_target_pairs={{0,8},{2,10},{4,12},{6,14},{8,0},{10,2},{12,4},{14,6},{16,24},{18,... | collective-permute-start | bytes 786440 | tf_op jit(solution)/shard_map/ppermute | solution.py:307
  54.1 14.6 %collective-permute-start.11 = (bf16[1,2,256,128]{3,2,1,0:T(8,128)(2,1)}, bf16[1,2,256,128]{3,2,1,0:T(8,128)(2,1)S(1)}, u32[]{:S(2)}, u32[]{:S(2)}) collective-permute-start(bf16[1,2,256,128]{3,2,1,0:T(8,128)(2,1)} %get-tuple-element.37), channel_id=1, source_target_pairs={{0,6},{2,4},{4,2},{6,0},{8,14},{10,12},{12,10},{14,8},{16,22},{18,... | collective-permute-start | bytes 393224 | tf_op jit(solution)/shard_map/ppermute | solution.py:307
  56.8 17.1 %collective-permute-start.12 = (bf16[1,2,256,128]{3,2,1,0:T(8,128)(2,1)}, bf16[1,2,256,128]{3,2,1,0:T(8,128)(2,1)S(1)}, u32[]{:S(2)}, u32[]{:S(2)}) collective-permute-start(bf16[1,2,256,128]{3,2,1,0:T(8,128)(2,1)} %get-tuple-element.38), channel_id=1, source_target_pairs={{0,2},{2,0},{4,6},{6,4},{8,10},{10,8},{12,14},{14,12},{16,18},{18,... | collective-permute-start | bytes 393224 | tf_op jit(solution)/shard_map/ppermute | solution.py:307
  56.9 19.8 %collective-permute-start.13 = (bf16[1,2,256,128]{3,2,1,0:T(8,128)(2,1)}, bf16[1,2,256,128]{3,2,1,0:T(8,128)(2,1)S(1)}, u32[]{:S(2)}, u32[]{:S(2)}) collective-permute-start(bf16[1,2,256,128]{3,2,1,0:T(8,128)(2,1)} %get-tuple-element.39), channel_id=1, source_target_pairs={{0,4},{2,6},{4,0},{6,2},{8,12},{10,14},{12,8},{14,10},{16,20},{18,... | collective-permute-start | bytes 393224 | tf_op jit(solution)/shard_map/ppermute | solution.py:307
  64.0 7.7 %collective-permute-start.19 = (bf16[256,512]{1,0:T(8,128)(2,1)S(1)}, bf16[256,512]{1,0:T(8,128)(2,1)S(1)}, u32[]{:S(2)}, u32[]{:S(2)}) collective-permute-start(bf16[256,512]{1,0:T(8,128)(2,1)S(1)} %collective-permute-done.15.refs_1_), channel_id=1, source_target_pairs={{0,8},{2,10},{4,12},{6,14},{8,0},{10,2},{12,4},{14,6},{16,24},{18,... | collective-permute-start | bytes 786440 | tf_op jit(solution)/shard_map/ppermute | solution.py:307
  65.7 11.7 %collective-permute-start.16 = (bf16[2,2,256,128]{3,2,1,0:T(8,128)(2,1)}, bf16[2,2,256,128]{3,2,1,0:T(8,128)(2,1)S(1)}, u32[]{:S(2)}, u32[]{:S(2)}) collective-permute-start(bf16[2,2,256,128]{3,2,1,0:T(8,128)(2,1)} %get-tuple-element.41), channel_id=1, source_target_pairs={{0,6},{2,4},{4,2},{6,0},{8,14},{10,12},{12,10},{14,8},{16,22},{18,... | collective-permute-start | bytes 786440 | tf_op jit(solution)/shard_map/ppermute | solution.py:307
  69.4 12.0 %collective-permute-start.17 = (bf16[2,2,256,128]{3,2,1,0:T(8,128)(2,1)}, bf16[2,2,256,128]{3,2,1,0:T(8,128)(2,1)S(1)}, u32[]{:S(2)}, u32[]{:S(2)}) collective-permute-start(bf16[2,2,256,128]{3,2,1,0:T(8,128)(2,1)} %get-tuple-element.42), channel_id=1, source_target_pairs={{0,2},{2,0},{4,6},{6,4},{8,10},{10,8},{12,14},{14,12},{16,18},{18,... | collective-permute-start | bytes 786440 | tf_op jit(solution)/shard_map/ppermute | solution.py:307
  71.6 12.3 %collective-permute-start.18 = (bf16[2,2,256,128]{3,2,1,0:T(8,128)(2,1)}, bf16[2,2,256,128]{3,2,1,0:T(8,128)(2,1)S(1)}, u32[]{:S(2)}, u32[]{:S(2)}) collective-permute-start(bf16[2,2,256,128]{3,2,1,0:T(8,128)(2,1)} %get-tuple-element.43), channel_id=1, source_target_pairs={{0,4},{2,6},{4,0},{6,2},{8,12},{10,14},{12,8},{14,10},{16,20},{18,... | collective-permute-start | bytes 786440 | tf_op jit(solution)/shard_map/ppermute | solution.py:307
  73.9 10.7 %collective-permute-start.20 = (bf16[1,2,256,128]{3,2,1,0:T(8,128)(2,1)}, bf16[1,2,256,128]{3,2,1,0:T(8,128)(2,1)S(1)}, u32[]{:S(2)}, u32[]{:S(2)}) collective-permute-start(bf16[1,2,256,128]{3,2,1,0:T(8,128)(2,1)} %get-tuple-element.45), channel_id=1, source_target_pairs={{0,6},{2,4},{4,2},{6,0},{8,14},{10,12},{12,10},{14,8},{16,22},{18,... | collective-permute-start | bytes 393224 | tf_op jit(solution)/shard_map/ppermute | solution.py:307
  76.7 9.2 %collective-permute-start.21 = (bf16[1,2,256,128]{3,2,1,0:T(8,128)(2,1)}, bf16[1,2,256,128]{3,2,1,0:T(8,128)(2,1)S(1)}, u32[]{:S(2)}, u32[]{:S(2)}) collective-permute-start(bf16[1,2,256,128]{3,2,1,0:T(8,128)(2,1)} %get-tuple-element.46), channel_id=1, source_target_pairs={{0,2},{2,0},{4,6},{6,4},{8,10},{10,8},{12,14},{14,12},{16,18},{18,... | collective-permute-start | bytes 393224 | tf_op jit(solution)/shard_map/ppermute | solution.py:307
  77.3 9.3 %collective-permute-start.22 = (bf16[1,2,256,128]{3,2,1,0:T(8,128)(2,1)}, bf16[1,2,256,128]{3,2,1,0:T(8,128)(2,1)}, u32[]{:S(2)}, u32[]{:S(2)}) collective-permute-start(bf16[1,2,256,128]{3,2,1,0:T(8,128)(2,1)} %get-tuple-element.47), channel_id=1, source_target_pairs={{0,4},{2,6},{4,0},{6,2},{8,12},{10,14},{12,8},{14,10},{16,20},{18,... | collective-permute-start | bytes 393224 | tf_op jit(solution)/shard_map/ppermute | solution.py:307
  (8 other events, 48.8 us)
